TPU v7x, 256 devices: a whole 4x4x8 slice. The times are simulated.
256 devices in a mesh: seq: 128 (over y, x, z), kmer: 2 (over core).
Axes of the slice: x: 4, y: 4, z: 8, core: 2. Of those that a mesh axis runs over, the one named last changes fastest.
Arguments:
- profiles: bfloat16 [2048, 131072], P(('seq', 'kmer')), may hold values from -6 to 6
- lengths: int32 [131072], P('seq'), may hold values from 64 to 1024
- owners: int32 [2], replicated, may hold values from 0 to 127
- block_mask: int32 [2, 1024, 8], P(None, 'seq'), may hold values 0 or 1
Outputs:
- scores: bfloat16 [131072, 2, 1024], P('seq', None, 'kmer')
All inputs are finite; a program needn't handle non-finite values. No bound on the sum of `block_mask` on one device may be relied on, other than what follows from the above.
Results may differ from a plain program's by a relative error of at most 0.001.
Values may be sent and summed in bfloat16 or wider, within the bound.
No kernel may reach another device: no remote copies, remote signals or barrier semaphores. Data moves between devices by JAX's collectives and lax.ppermute only.
A program may use at most 64 MiB of HBM per device.

v0:
```python
import jax
import jax.numpy as jnp
from jax import lax
from jax.sharding import PartitionSpec as P

KM = 2048
BLK = 128
SECTIONS = 2


def broadcast(block, axis, source):
    block = jnp.where(lax.axis_index(axis) == source, block, jnp.zeros_like(block))
    return lax.psum(block, axis)


def shards(profiles, lengths, owners, block_mask):
    local = lax.all_to_all(profiles, "seq", split_axis=1, concat_axis=0, tiled=True)
    panel_rows = local.shape[1]
    half = panel_rows // 2
    part = lax.axis_index("kmer")
    row_len = lengths.astype(jnp.float32)
    scale = 256.0 / jnp.sqrt(jnp.float32(KM))
    contract = (((0,), (0,)), ((), ()))
    outs = []
    for section in range(SECTIONS):
        panel, panel_len = (
            broadcast(local, "seq", owners[section]),
            broadcast(lengths, "seq", owners[section]),
        )
        partial_value = lax.dot_general(local, panel, contract, preferred_element_type=jnp.float32)
        raw = lax.psum_scatter(partial_value, "kmer", scatter_dimension=1, tiled=True)
        col_len = lax.dynamic_slice_in_dim(panel_len.astype(jnp.float32), part * half, half, 0)
        mask_full = jnp.repeat(jnp.repeat(block_mask[section], BLK, axis=0), BLK, axis=1).astype(
            jnp.float32
        )
        mask = lax.dynamic_slice_in_dim(mask_full, part * half, half, 1)
        norm = scale * lax.rsqrt(row_len[:, None] * col_len[None, :])
        outs.append((raw * norm * mask).astype(jnp.bfloat16))
    return jnp.stack(outs, axis=1)


def solution(mesh):
    placed = (P(("seq", "kmer"), None), P("seq"), P(), P(None, "seq", None))
    return jax.shard_map(
        shards, mesh=mesh, in_specs=placed, out_specs=P("seq", None, "kmer"), check_vma=False
    )
```

profile of v0, /device:TPU:1, one launch (start us, length us, event | category | flops | bytes accessed | tf_op | source)
XLA Modules:
  0.0 364.0 jit_solution(3073027585072438765)
XLA Ops:
  6.5 0.0 copy-start.4
  6.5 16.5 %all-to-all-start = ((bf16[8,128,1024]{2,0,1:T(8,128)(2,1)}), bf16[8,128,1024]{2,0,1:T(8,128)(2,1)S(1)}, u32[]{:S(2)}, u32[]{:S(2)}) async-start(bf16[8,128,1024]{2,0,1:T(8,128)(2,1)} %bitcast.34), calls=%async_computation | async-start | bytes 4194304 | tf_op jit(solution)/shard_map/all_to_all | solution.py:17
  23.0 0.0 all-reduce.4.cloned.1.call-start
  23.1 0.0 copy-done.4
  23.1 0.6 fusion.5
  24.9 50.8 %all-to-all-done = bf16[8,128,1024]{2,0,1:T(8,128)(2,1)S(1)} async-done(((bf16[8,128,1024]{2,0,1:T(8,128)(2,1)}), bf16[8,128,1024]{2,0,1:T(8,128)(2,1)S(1)}, u32[]{:S(2)}, u32[]{:S(2)}) %all-to-all-start) | async-done | bytes 2097184 | tf_op jit(solution)/shard_map/all_to_all | solution.py:17
  75.7 2.3 bitcast_select_fusion.1
  78.0 0.0 all-reduce.4.cloned.1.call-update
  78.0 0.0 reduce-scatter.3.cloned.1.call-start
  78.1 225.4 %all-reduce.4.cloned.1.call-done = (bf16[1024,1024]{1,0:T(8,128)(2,1)}, bf16[1024,1024]{1,0:T(8,128)(2,1)}) async-done(((bf16[1024,1024]{1,0:T(8,128)(2,1)}, bf16[1024,1024]{1,0:T(8,128)(2,1)}), (bf16[1024,1024]{1,0:T(8,128)(2,1)}, bf16[1024,1024]{1,0:T(8,128)(2,1)})) %all-reduce.4.cloned.1.call-update) | async-done | bytes 4194320 | tf_op jit(solution)/shard_map/psum | solution.py:13
  303.5 5.9 %convolution_bitcast_fusion.1 = f32[1024,1024]{0,1:T(8,128)} fusion(bf16[1024,1024]{1,0:T(8,128)(2,1)} %get-tuple-element.8, bf16[8,128,1024]{2,0,1:T(8,128)(2,1)S(1)} %all-to-all-done), kind=kOutput, calls=%fused_computation.1 | convolution fusion | flops 2147483648 | bytes 8388608 | tf_op jit(solution)/shard_map/dot_general | solution.py:30
  309.4 0.0 reduce-scatter.3.cloned.1.call-update
  309.4 0.0 reduce-scatter.5.cloned.1.call-start
  309.5 5.9 %convolution_bitcast_fusion = f32[1024,1024]{0,1:T(8,128)} fusion(bf16[1024,1024]{1,0:T(8,128)(2,1)} %get-tuple-element.7, bf16[8,128,1024]{2,0,1:T(8,128)(2,1)S(1)} %all-to-all-done), kind=kOutput, calls=%fused_computation | convolution fusion | flops 2147483648 | bytes 8388608 | tf_op jit(solution)/shard_map/dot_general | solution.py:30
  315.4 0.0 copy-start.3
  315.4 0.0 copy-start.2
  315.5 0.0 reduce-scatter.5.cloned.1.call-update
  315.5 0.7 copy-done.3
  316.1 20.1 %all-reduce = (s32[1024]{0:T(1024)S(1)}, s32[1024]{0:T(1024)S(1)}) all-reduce(s32[1024]{0:T(1024)S(1)} %get-tuple-element.16, s32[1024]{0:T(1024)S(1)} %get-tuple-element.17), channel_id=1, replica_groups=mesh['seq'=128,'kmer'=2] {'seq'}, use_global_device_ids=true, to_apply=%region_5.6 | all-reduce | flops 2048 | bytes 16384 | tf_op jit(solution)/shard_map/psum | solution.py:13
  336.2 0.1 dynamic_slice.12
  336.3 0.1 dynamic_slice.14
  336.4 0.0 copy-done.2
  336.4 0.1 broadcast_bitcast_fusion
  336.4 0.0 reduce-scatter.3.cloned.1.call-done
  336.5 13.2 %reduce-scatter.5.cloned.1.call-done = f32[1024,512]{0,1:T(8,128)} async-done(((f32[1024,1024]{0,1:T(8,128)}), f32[1024,512]{0,1:T(8,128)}) %reduce-scatter.5.cloned.1.call-update) | async-done | bytes 2097168 | tf_op jit(solution)/shard_map/reduce_scatter | solution.py:31
  349.7 0.5 broadcast_in_dim.19
  350.2 0.0 copy-start
  350.2 0.0 copy-start.1
  350.2 0.5 broadcast_in_dim.17
  350.7 1.1 copy-done
  351.8 0.6 copy-done.1
  352.4 0.8 fusion.2
  353.3 0.2 pad_maximum_fusion
  353.5 4.0 %copy.5 = bf16[1024,2,512]{2,1,0:T(2,128)(2,1)} copy(bf16[1024,2,512]{0,2,1:T(8,128)(2,1)S(1)} %pad_maximum_fusion) | data formatting | bytes 4194304 | tf_op jit(solution)/shard_map/stack | solution.py:39
  (4 shorter events, 0.0 us)
Async XLA Ops:
  6.5 16.5 %copy-start.4 = (s32[2]{0:T(128)S(1)}, s32[2]{0:T(128)}, u32[]{:S(2)}) copy-start(s32[2]{0:T(128)} %param.6) | copy-start | bytes 28
  6.5 69.2 %all-to-all-start = ((bf16[8,128,1024]{2,0,1:T(8,128)(2,1)}), bf16[8,128,1024]{2,0,1:T(8,128)(2,1)S(1)}, u32[]{:S(2)}, u32[]{:S(2)}) async-start(bf16[8,128,1024]{2,0,1:T(8,128)(2,1)} %bitcast.34), calls=%async_computation | async-start | bytes 4194304 | tf_op jit(solution)/shard_map/all_to_all | solution.py:17
  23.0 280.5 %all-reduce.4.cloned.1.call-start = ((), (), s32[]{:S(2)}) async-start(), calls=%async_computation.5 | async-start | bytes 8388608 | tf_op jit(solution)/shard_map/psum | solution.py:13
  78.0 258.4 %reduce-scatter.3.cloned.1.call-start = ((), (), s32[]{:S(2)}) async-start(), calls=%async_computation.3 | async-start | bytes 6291456 | tf_op jit(solution)/shard_map/reduce_scatter | solution.py:31
  309.4 40.2 %reduce-scatter.5.cloned.1.call-start = ((), (), s32[]{:S(2)}) async-start(), calls=%async_computation.4 | async-start | bytes 6291456 | tf_op jit(solution)/shard_map/reduce_scatter | solution.py:31
  315.4 0.7 copy-start.3
  315.4 20.9 %copy-start.2 = (s32[2,8,8]{2,1,0:T(8,128)S(1)}, s32[2,8,8]{2,1,0:T(8,128)}, u32[]{:S(2)}) copy-start(s32[2,8,8]{2,1,0:T(8,128)} %param.7) | copy-start | bytes 1540
  350.2 1.6 copy-start
  350.2 2.2 copy-start.1
Sparse Core Ops, SparseCore 0:
  78.1 225.3 all-reduce.3
  309.6 18.6 reduce-scatter.2
  330.9 18.7 reduce-scatter.4
where the time goes:
time: 364 us
  waiting for transfers between devices  290 us (80%)
  blocking collectives  20.1 us (6%)
  starting transfers between devices  16.6 us (5%)
  between operations  14.4 us (4%)
  matrix products  11.9 us (3%)
  local copies, waits for them, and re-layouts  8.25 us (2%)
    psum x1, waiting for transfers between devices, broadcast(): return lax.psum(block, axis)  225 us
    all_to_all x1, waiting for transfers between devices, shards(): lax.all_to_all(profiles, 'seq', split_axis=1, concat_axis=0, tiled=True)  50.8 us
    psum x1, blocking collectives, broadcast(): return lax.psum(block, axis)  20.1 us
    all_to_all x1, starting transfers between devices, shards(): lax.all_to_all(profiles, 'seq', split_axis=1, concat_axis=0, tiled=True)  16.5 us
    reduce_scatter x2, waiting for transfers between devices, shards(): lax.psum_scatter(partial_value, 'kmer', scatter_dimension=1, tiled=True)  13.2 us
    dot_general x2, matrix products, shards(): lax.dot_general(local, panel, contract, preferred_element_type=jnp.float32)  11.9 us
  transfers between devices with their start and end apart: 4, of which 3 were waited for; matrix products, arithmetic and copies ran while one was open for 2% of the time, Pallas kernels for 0%

commit v1 on v0

v1 whole, which is shorter than its diff:
```python
import jax
import jax.numpy as jnp
from jax import lax
from jax.experimental import pallas as pl
from jax.experimental.pallas import tpu as pltpu
from jax.sharding import PartitionSpec as P

KM = 2048
PANEL = 1024
BLK = 128
SECTIONS = 2
HALF = PANEL // 2
WIDTH = SECTIONS * HALF
SWAP = [(0, 1), (1, 0)]
NY, NX, NZ = 4, 4, 8
LINES = [[yx * NZ + z for z in range(NZ)] for yx in range(NY * NX)]
FEATURES = 8
RUN = NZ * FEATURES
GROUP = 4 * RUN
LENS = 16
SCALE = 256.0 / KM**0.5
ROWS = 256
VMEM = pl.BlockSpec(memory_space=pltpu.VMEM)
SMEM = pl.BlockSpec(memory_space=pltpu.SMEM)
CONTRACT = (((0,), (0,)), ((), ()))


def params(mebibytes):
    return pltpu.CompilerParams(vmem_limit_bytes=mebibytes << 20)


def number(y, x, z):
    return (y % NY * NX + x % NX) * NZ + z


def shift(value, turn, by):
    pairs = []
    for y in range(NY):
        for x in range(NX):
            for z in range(NZ):
                for core in range(2):
                    to = number(y, x + by, z) if core == turn else number(y + by, x, z)
                    pairs.append((number(y, x, z) * 2 + core, to * 2 + core))
    return lax.ppermute(value, ("seq", "kmer"), pairs)


def swap(value):
    return lax.ppermute(value, "kmer", SWAP)


def piece_kernel(own_ref, place_ref, a_ref, b_ref, c_ref, d_ref, len_ref, out_ref):
    seq = place_ref[0]
    for i, ref in enumerate((a_ref, b_ref, c_ref, d_ref)):
        out_ref[:, :, i * HALF : (i + 1) * HALF] = jnp.broadcast_to(ref[...][None], (NZ, FEATURES, HALF))
    size = len_ref[...].reshape(1, HALF)
    rows = [jnp.where(own_ref[t] == seq, size, 0) for t in range(SECTIONS)]
    for i in range(2):
        parts = []
        for t in range(SECTIONS):
            value = jnp.right_shift(rows[t], 8) if i == 0 else jnp.bitwise_and(rows[t], 255)
            value = value.astype(jnp.float32)
            parts += [value[:, j * BLK : (j + 1) * BLK] for j in range(HALF // BLK)]
        tile = jnp.concatenate(parts, axis=0).astype(jnp.bfloat16)
        at = 2 * WIDTH + i * BLK
        out_ref[:, :, at : at + BLK] = jnp.broadcast_to(tile[None], (NZ, FEATURES, BLK))


def make_piece(owners, place, profiles, lengths):
    def spec(t, other):
        def index(i, own, at):
            return 0, own[t] * 2 + (1 - at[1] if other else at[1])

        return pl.BlockSpec((FEATURES, HALF), index)

    shape = (NZ, FEATURES, 2 * WIDTH + 2 * BLK)
    return pl.pallas_call(
        piece_kernel,
        grid_spec=pltpu.PrefetchScalarGridSpec(
            num_scalar_prefetch=2,
            grid=(1,),
            in_specs=[
                spec(0, False),
                spec(1, False),
                spec(0, True),
                spec(1, True),
                pl.BlockSpec((HALF,), lambda i, own, at: (at[1],)),
            ],
            out_specs=pl.BlockSpec(shape, lambda i, own, at: (0, 0, 0)),
        ),
        out_shape=jax.ShapeDtypeStruct(shape, jnp.bfloat16),
    )(owners, place, profiles, profiles, profiles, profiles, lengths)


def line_kernel(line_ref, out_ref):
    for i in range(0, NZ, 2):
        out_ref[i * FEATURES : (i + 2) * FEATURES, : 2 * WIDTH] = jnp.concatenate(
            [line_ref[i, :, : 2 * WIDTH], line_ref[i + 1, :, : 2 * WIDTH]], axis=0
        )
    lens = jnp.sum(line_ref[:, :, 2 * WIDTH :].astype(jnp.float32), axis=0)
    lens = jnp.concatenate([lens[:, :BLK], lens[:, BLK:], jnp.zeros((RUN - LENS, BLK), jnp.float32)], axis=0)
    out_ref[:, 2 * WIDTH :] = lens.astype(jnp.bfloat16)


def make_line(line):
    return pl.pallas_call(
        line_kernel,
        in_specs=[VMEM],
        out_specs=VMEM,
        out_shape=jax.ShapeDtypeStruct((RUN, 2 * WIDTH + BLK), jnp.bfloat16),
        compiler_params=params(6),
    )(line)


def group_kernel(a_ref, b_ref, c_ref, d_ref, mine_ref, other_ref):
    lens = jnp.zeros((LENS, BLK), jnp.float32)
    for i, ref in enumerate((a_ref, b_ref, c_ref, d_ref)):
        mine_ref[i * RUN : (i + 1) * RUN] = ref[:, :WIDTH]
        other_ref[i * RUN : (i + 1) * RUN] = ref[:, WIDTH : 2 * WIDTH]
        lens = lens + ref[:LENS, 2 * WIDTH :].astype(jnp.float32)
    mine_ref[GROUP:] = jnp.concatenate([lens] * (WIDTH // BLK), axis=1).astype(jnp.bfloat16)


def make_group(*blocks):
    return pl.pallas_call(
        group_kernel,
        in_specs=[VMEM] * 4,
        out_specs=[VMEM] * 2,
        out_shape=[
            jax.ShapeDtypeStruct((GROUP + LENS, WIDTH), jnp.bfloat16),
            jax.ShapeDtypeStruct((GROUP, WIDTH), jnp.bfloat16),
        ],
        compiler_params=params(6),
    )(*blocks)


def pack_kernel(*refs):
    panels, swapped, (own_ref, other_ref, len_ref) = refs[:4], refs[4:8], refs[8:]
    for i in range(4):
        own_ref[i * GROUP : (i + 1) * GROUP] = panels[i][:GROUP]
        other_ref[i * GROUP : (i + 1) * GROUP] = swapped[i][...]
    lens = sum(ref[GROUP:, :BLK].astype(jnp.float32) for ref in panels)
    lens = lens[:8] * 256 + lens[8:]
    len_ref[...] = jnp.concatenate([lens[j : j + 1] for j in range(8)], axis=1)


def pack(panels, swapped):
    whole = jax.ShapeDtypeStruct((4 * GROUP, WIDTH), jnp.bfloat16)
    return pl.pallas_call(
        pack_kernel,
        in_specs=[VMEM] * 8,
        out_specs=[VMEM] * 3,
        out_shape=[whole, whole, jax.ShapeDtypeStruct((1, WIDTH), jnp.float32)],
        compiler_params=params(6),
    )(*panels, *swapped)


def product(at_ref, rows_ref, panel_ref, x_inside, columns):
    y, x = at_ref[2], at_ref[3]
    parts = []
    for outer in range(4):
        for inner in range(4):
            ry = jnp.where(x_inside, outer, inner)
            rx = jnp.where(x_inside, inner, outer)
            source = jnp.bitwise_and(y - ry, NY - 1) * NX + jnp.bitwise_and(x - rx, NX - 1)
            parts.append(rows_ref[pl.ds(pl.multiple_of(source * RUN, RUN), RUN), columns])
    rows = jnp.concatenate(parts, axis=0)
    return lax.dot_general(rows, panel_ref[...], CONTRACT, preferred_element_type=jnp.float32)


def first_kernel(at_ref, rows_ref, panel_ref, out_ref):
    for i in range(PANEL // ROWS):
        columns = slice(i * ROWS, (i + 1) * ROWS)
        out_ref[columns, :] = product(at_ref, rows_ref, panel_ref, at_ref[1] == 0, columns)


def first_dot(place, local, panel):
    return pl.pallas_call(
        first_kernel,
        in_specs=[SMEM] + [VMEM] * 2,
        out_specs=VMEM,
        out_shape=jax.ShapeDtypeStruct((PANEL, WIDTH), jnp.float32),
        compiler_params=params(20),
        cost_estimate=pl.CostEstimate(flops=2 << 30, bytes_accessed=8 << 20, transcendentals=0),
    )(place, local, panel)


def second_kernel(
    at_ref, rows_ref, panel_ref, total_ref, col_len_ref, len_ref, mask_ref, out_ref, ready, sems
):
    left = at_ref[1] == 0
    col_len = col_len_ref[...]
    row_lens = len_ref[...].astype(jnp.float32).T
    side = HALF // BLK
    mask = jnp.concatenate(
        [jnp.where(left, mask_ref[t, :, :side], mask_ref[t, :, side:]) for t in range(SECTIONS)], axis=1
    ).astype(jnp.float32)
    row = lax.broadcasted_iota(jnp.int32, (2 * BLK, 2 * BLK), 0)
    column = lax.broadcasted_iota(jnp.int32, (2 * BLK, 2 * BLK), 1)
    at = jnp.bitwise_and(row, 1) * BLK + jnp.right_shift(row, 1)
    order = (column == at).astype(jnp.float32).astype(jnp.bfloat16)
    copies = []
    for i in range(PANEL // ROWS):
        columns = slice(i * ROWS, (i + 1) * ROWS)
        raw = product(at_ref, rows_ref, panel_ref, at_ref[1] == 1, columns) + total_ref[columns, :]
        for h in range(ROWS // BLK):
            b = i * (ROWS // BLK) + h
            norm = SCALE * lax.rsqrt(row_lens[:, b : b + 1] * col_len)
            spread = jnp.concatenate(
                [jnp.broadcast_to(mask[b : b + 1, j : j + 1], (BLK, BLK)) for j in range(WIDTH // BLK)], axis=1
            )
            scores = (raw[h * BLK : (h + 1) * BLK] * norm * spread).astype(jnp.bfloat16)
            stacked = jnp.concatenate([scores[:, :HALF], scores[:, HALF:]], axis=0)
            mixed = jnp.dot(order, stacked, preferred_element_type=jnp.float32).astype(jnp.bfloat16)
            ready[b * BLK : (b + 1) * BLK] = mixed.reshape(BLK, SECTIONS, HALF)
        copy = pltpu.make_async_copy(ready.at[columns], out_ref.at[columns], sems.at[i])
        copy.start()
        copies.append(copy)
    for copy in copies:
        copy.wait()


def second_dot(place, remote, panel, total, col_len, lengths, mask):
    return pl.pallas_call(
        second_kernel,
        in_specs=[SMEM] + [VMEM] * 6,
        out_specs=pl.BlockSpec(memory_space=pl.ANY),
        out_shape=jax.ShapeDtypeStruct((PANEL, SECTIONS, HALF), jnp.bfloat16),
        scratch_shapes=[
            pltpu.VMEM((PANEL, SECTIONS, HALF), jnp.bfloat16),
            pltpu.SemaphoreType.DMA((PANEL // ROWS,)),
        ],
        compiler_params=params(20),
        cost_estimate=pl.CostEstimate(flops=2 << 30, bytes_accessed=8 << 20, transcendentals=0),
    )(place, remote, panel, total, col_len, lengths, mask)


def shards(profiles, lengths, owners, block_mask):
    part = lax.axis_index("kmer")
    seq = lax.axis_index("seq")
    y, x = seq // (NX * NZ), seq // NZ % NX
    place = jnp.stack([seq, part, y, x]).astype(jnp.int32)
    piece = make_piece(owners, place, profiles, lengths)
    line = lax.all_to_all(piece, "seq", 0, 0, axis_index_groups=LINES, tiled=True)
    line, profiles = lax.optimization_barrier((line, profiles))
    local = lax.all_to_all(profiles, "seq", split_axis=1, concat_axis=0, tiled=True)

    line = make_line(line)
    mine, other = make_group(line, *[shift(line, 0, by) for by in (1, 2, 3)])
    mine_up, other_down = shift(mine, 1, 1), shift(other, 1, -1)
    other_up, mine_down = shift(other, 1, 1), shift(mine, 1, -1)
    mine_far, other_far = shift(mine_up, 1, 1), shift(other_down, 1, -1)
    panels = [mine, mine_up, mine_far, mine_down]
    swapped = [swap(a) for a in (other, other_up, other_far, other_down)]
    own_panel, other_panel, col_len = pack(panels, swapped)
    local, own_panel, other_panel, col_len = lax.optimization_barrier((local, own_panel, other_panel, col_len))
    remote = swap(local)
    total = first_dot(place, local, own_panel)
    return second_dot(place, remote, other_panel, total, col_len, lengths.reshape(PANEL // BLK, BLK), block_mask)


def solution(mesh):
    placed = (P(("seq", "kmer"), None), P("seq"), P(), P(None, "seq", None))
    return jax.shard_map(
        shards, mesh=mesh, in_specs=placed, out_specs=P("seq", None, "kmer"), check_vma=False
    )
```

time: 364 us -> 101 us (0.28)
  waiting for transfers between devices: 290 us -> 38.2 us
  between operations: 14.4 us -> 0.25 us
  matrix products: 11.9 us -> 0 us
  Pallas kernels: 0 us -> 10.7 us
  starting transfers between devices: 16.6 us -> 26.8 us
  local copies, waits for them, and re-layouts: 8.25 us -> 4.26 us
    psum x1 -> x0, waiting for transfers between devices: 225 us -> none  [broadcast(): return lax.psum(block, axis)]
    all_to_all x1, waiting for transfers between devices: 50.8 us -> 0.01 us  [shards(): lax.all_to_all(profiles, 'seq', split_axis=1, concat_axis=0, tiled=True)]
    ppermute x0 -> x14, waiting for transfers between devices: none -> 38.2 us  [the longest x9 38.2 us: shift(): return lax.ppermute(value, ('seq', 'kmer'), pairs)]
    psum x1 -> x0, blocking collectives: 20.1 us -> none  [broadcast(): return lax.psum(block, axis)]
    all_to_all x0 -> x1, blocking collectives: none -> 19.9 us  [shards(): lax.all_to_all(piece, 'seq', 0, 0, axis_index_groups=LINES, tiled=True)]
    ppermute x0 -> x14, starting transfers between devices: none -> 16.4 us  [the longest x9 11.2 us: shift(): return lax.ppermute(value, ('seq', 'kmer'), pairs)]
    reduce_scatter x2 -> x0, waiting for transfers between devices: 13.2 us -> none  [shards(): lax.psum_scatter(partial_value, 'kmer', scatter_dimension=1, tiled=True)]
    dot_general x2 -> x0, matrix products: 11.9 us -> none  [shards(): lax.dot_general(local, panel, contract, preferred_element_type=jnp.float32)]
  transfers between devices with their start and end apart: 4 -> 15, of which waited for: 3 -> 6; matrix products, arithmetic and copies ran while one was open for 2% -> 0% of each run, Pallas kernels for 0% -> 3%
where the time goes in v1:
time: 101 us
  waiting for transfers between devices  38.2 us (38%)
  starting transfers between devices  26.8 us (27%)
  blocking collectives  19.9 us (20%)
  Pallas kernels  10.7 us (11%)
  local copies, waits for them, and re-layouts  4.26 us (4%)
    ppermute x9, waiting for transfers between devices, shift(): return lax.ppermute(value, ('seq', 'kmer'), pairs)  38.2 us
    all_to_all x1, blocking collectives, shards(): lax.all_to_all(piece, 'seq', 0, 0, axis_index_groups=LINES, tiled=True)  19.9 us
    ppermute x9, starting transfers between devices, shift(): return lax.ppermute(value, ('seq', 'kmer'), pairs)  11.2 us
    all_to_all x1, starting transfers between devices, shards(): lax.all_to_all(profiles, 'seq', split_axis=1, concat_axis=0, tiled=True)  10.5 us
    ppermute x5, starting transfers between devices, swap(): return lax.ppermute(value, 'kmer', SWAP)  5.2 us
    pallas_call x1, Pallas kernels, second_dot(): pl.pallas_call(second_kernel, in_specs=[SMEM] + [VMEM] * 6, out_specs=pl....  5.15 us
    unnamed x14, local copies, waits for them, and re-layouts  4.26 us
    pallas_call x1, Pallas kernels, first_dot(): pl.pallas_call(first_kernel, in_specs=[SMEM] + [VMEM] * 2, out_specs=VMEM...  2.96 us
  transfers between devices with their start and end apart: 15, of which 6 were waited for; matrix products, arithmetic and copies ran while one was open for 0% of the time, Pallas kernels for 3%

profile of v1, /device:TPU:1, one launch (start us, length us, event | category | flops | bytes accessed | tf_op | source)
XLA Modules:
  0.0 100.8 jit_solution(17186890957234703131)
XLA Ops:
  0.0 0.7 pad_add_fusion.place_ref.at_ref
  0.7 2.2 %shard_map.46 = bf16[8,8,2304]{2,1,0:T(8,128)(2,1)} custom-call(s32[2]{0:T(128)} %own_ref.1, s32[4]{0:T(128)} %pad_add_fusion.place_ref.at_ref, bf16[8,131072]{1,0:T(8,128)(2,1)} %d_ref.1, bf16[8,131072]{1,0:T(8,128)(2,1)} %d_ref.1, bf16[8,131072]{1,0:T(8,128)(2,1)} %d_ref.1, bf16[8,131072]{1,0:T(8,128)(2,1)} %d_ref.1, s32[1024]{0:T(1024)} %len_ref.1), custom_call_target="tpu_custom_call" | custom-call | tf_op jit(solution)/shard_map/pallas_call | solution.py:76
  2.8 19.9 %all_to_all.24.line_ref = bf16[8,8,2304]{2,1,0:T(8,128)(2,1)S(1)} all-to-all(bf16[8,8,2304]{2,1,0:T(8,128)(2,1)} %shard_map.46), channel_id=1, replica_groups={{0,2,4,6,8,10,12,14},{16,18,20,22,24,26,28,30},{32,34,36,38,40,42,44,46..., dimensions={0} | all-to-all | bytes 589824 | tf_op jit(solution)/shard_map/all_to_all | solution.py:243
  22.7 10.5 %all-to-all-start.1 = ((bf16[8,128,1024]{2,0,1:T(8,128)(2,1)}), bf16[8,128,1024]{2,0,1:T(8,128)(2,1)S(1)}, u32[]{:S(2)}, u32[]{:S(2)}) async-start(bf16[8,128,1024]{2,0,1:T(8,128)(2,1)} %bitcast.12), calls=%async_computation.1 | async-start | bytes 4194304 | tf_op jit(solution)/shard_map/all_to_all | solution.py:245
  33.2 0.8 collective-permute-start
  34.0 2.8 %collective-permute-start.1 = (bf16[64,2176]{1,0:T(8,128)(2,1)S(1)}, bf16[64,2176]{1,0:T(8,128)(2,1)S(1)}, u32[]{:S(2)}, u32[]{:S(2)}) collective-permute-start(bf16[64,2176]{1,0:T(8,128)(2,1)S(1)} %shard_map.47.a_ref), channel_id=1, source_target_pairs={{0,32},{1,129},{2,34},{3,131},{4,36},{5,133},{6,38},{7,135},{8,40}... | collective-permute-start | bytes 835592 | tf_op jit(solution)/shard_map/ppermute | solution.py:44
  36.8 1.0 collective-permute-start.2
  37.8 7.1 %collective-permute-done.b_ref = bf16[64,2176]{1,0:T(8,128)(2,1)S(1)} collective-permute-done((bf16[64,2176]{1,0:T(8,128)(2,1)S(1)}, bf16[64,2176]{1,0:T(8,128)(2,1)S(1)}, u32[]{:S(2)}, u32[]{:S(2)}) %collective-permute-start) | collective-permute-done | bytes 278560 | tf_op jit(solution)/shard_map/ppermute | solution.py:44
  44.9 6.7 %collective-permute-done.1.c_ref = bf16[64,2176]{1,0:T(8,128)(2,1)S(1)} collective-permute-done((bf16[64,2176]{1,0:T(8,128)(2,1)S(1)}, bf16[64,2176]{1,0:T(8,128)(2,1)S(1)}, u32[]{:S(2)}, u32[]{:S(2)}) %collective-permute-start.1) | collective-permute-done | bytes 278560 | tf_op jit(solution)/shard_map/ppermute | solution.py:44
  51.6 0.0 collective-permute-done.2.d_ref
  51.6 0.1 shard_map.48
  51.7 1.6 %collective-permute-start.9 = (bf16[256,1024]{1,0:T(8,128)(2,1)S(1)}, bf16[256,1024]{1,0:T(8,128)(2,1)S(1)}, u32[]{:S(2)}, u32[]{:S(2)}) collective-permute-start(bf16[256,1024]{1,0:T(8,128)(2,1)S(1)} %get-tuple-element.19), channel_id=1, source_target_pairs={{0,192},{1,49},{2,194},{3,51},{4,196},{5,53},{6,198},{7,55},{8,200... | collective-permute-start | bytes 1572872 | tf_op jit(solution)/shard_map/ppermute | solution.py:44
  53.2 0.0 copy-start.6
  53.2 0.2 collective-permute-start.3
  53.5 1.4 %collective-permute-start.7 = (bf16[256,1024]{1,0:T(8,128)(2,1)S(1)}, bf16[256,1024]{1,0:T(8,128)(2,1)S(1)}, u32[]{:S(2)}, u32[]{:S(2)}) collective-permute-start(bf16[256,1024]{1,0:T(8,128)(2,1)S(1)} %get-tuple-element.19), channel_id=1, source_target_pairs={{0,64},{1,17},{2,66},{3,19},{4,68},{5,21},{6,70},{7,23},{8,72},{9,... | collective-permute-start | bytes 1572872 | tf_op jit(solution)/shard_map/ppermute | solution.py:44
  54.8 0.3 collective-permute-start.6
  55.2 9.8 %collective-permute-done.9 = bf16[256,1024]{1,0:T(8,128)(2,1)S(1)} collective-permute-done((bf16[256,1024]{1,0:T(8,128)(2,1)S(1)}, bf16[256,1024]{1,0:T(8,128)(2,1)S(1)}, u32[]{:S(2)}, u32[]{:S(2)}) %collective-permute-start.9) | collective-permute-done | bytes 524320 | tf_op jit(solution)/shard_map/ppermute | solution.py:44
  65.0 2.0 %collective-permute-start.10 = (bf16[256,1024]{1,0:T(8,128)(2,1)S(1)}, bf16[256,1024]{1,0:T(8,128)(2,1)S(1)}, u32[]{:S(2)}, u32[]{:S(2)}) collective-permute-start(bf16[256,1024]{1,0:T(8,128)(2,1)S(1)} %collective-permute-done.9), channel_id=1, source_target_pairs={{0,192},{1,49},{2,194},{3,51},{4,196},{5,53},{6,198},{7,55},{8,200... | collective-permute-start | bytes 1572872 | tf_op jit(solution)/shard_map/ppermute | solution.py:44
  67.0 0.8 collective-permute-start.5
  67.8 0.0 collective-permute-done.3.refs_1_
  67.8 0.6 collective-permute-start.4
  68.5 9.4 %collective-permute-done.7 = bf16[256,1024]{1,0:T(8,128)(2,1)S(1)} collective-permute-done((bf16[256,1024]{1,0:T(8,128)(2,1)S(1)}, bf16[256,1024]{1,0:T(8,128)(2,1)S(1)}, u32[]{:S(2)}, u32[]{:S(2)}) %collective-permute-start.7) | collective-permute-done | bytes 524320 | tf_op jit(solution)/shard_map/ppermute | solution.py:44
  77.9 2.4 %collective-permute-start.12 = (bf16[256,1024]{1,0:T(8,128)(2,1)S(1)}, bf16[256,1024]{1,0:T(8,128)(2,1)S(1)}, u32[]{:S(2)}, u32[]{:S(2)}) collective-permute-start(bf16[256,1024]{1,0:T(8,128)(2,1)S(1)} %collective-permute-done.9), channel_id=1, source_target_pairs={{0,1},{1,0},{2,3},{3,2},{4,5},{5,4},{6,7},{7,6},{8,9},{9,8},{10,11... | collective-permute-start | bytes 1572872 | tf_op jit(solution)/shard_map/ppermute | solution.py:48
  80.2 0.0 collective-permute-done.6.refs_4_
  80.2 0.0 collective-permute-start.8
  80.2 0.0 collective-permute-done.10
  80.2 0.5 collective-permute-start.11
  80.7 4.2 %collective-permute-done.5.refs_3_ = bf16[272,1024]{1,0:T(8,128)(2,1)S(1)} collective-permute-done((bf16[272,1024]{1,0:T(8,128)(2,1)S(1)}, bf16[272,1024]{1,0:T(8,128)(2,1)S(1)}, u32[]{:S(2)}, u32[]{:S(2)}) %collective-permute-start.5) | collective-permute-done | bytes 557088 | tf_op jit(solution)/shard_map/ppermute | solution.py:44
  85.0 0.0 collective-permute-done.12.refs_7_
  85.0 0.0 collective-permute-done.8.refs_5_
  85.0 1.0 collective-permute-done.4.refs_2_
  86.0 0.0 collective-permute-done.11.refs_6_
  86.0 0.3 shard_map.49
  86.2 0.0 copy-start
  86.3 1.3 %copy-done = bf16[1024,1024]{1,0:T(8,128)(2,1)} copy-done((bf16[1024,1024]{1,0:T(8,128)(2,1)}, bf16[1024,1024]{1,0:T(8,128)(2,1)S(1)}, u32[]{:S(2)}) %copy-start) | copy-done | bytes 2097176
  87.6 0.0 copy-start.2
  87.6 1.3 %copy-done.2 = bf16[1024,1024]{1,0:T(8,128)(2,1)} copy-done((bf16[1024,1024]{1,0:T(8,128)(2,1)}, bf16[1024,1024]{1,0:T(8,128)(2,1)S(1)}, u32[]{:S(2)}) %copy-start.2) | copy-done | bytes 2097176
  88.9 0.0 all-to-all-done.1
  88.9 0.0 copy-start.1
  88.9 2.0 %collective-permute-start.13 = (bf16[1024,1024]{1,0:T(8,128)(2,1)S(1)}, bf16[1024,1024]{1,0:T(8,128)(2,1)S(1)}, u32[]{:S(2)}, u32[]{:S(2)}) collective-permute-start(bf16[1024,1024]{1,0:T(8,128)(2,1)S(1)} %bitcast.9), channel_id=1, source_target_pairs={{0,1},{1,0},{2,3},{3,2},{4,5},{5,4},{6,7},{7,6},{8,9},{9,8},{10,11... | collective-permute-start | bytes 6291464 | tf_op jit(solution)/shard_map/ppermute | solution.py:48
  90.9 0.0 copy-done.6
  90.9 0.0 copy-start.3
  90.9 1.6 %copy-done.3 = bf16[1024,1024]{1,0:T(8,128)(2,1)S(1)} copy-done((bf16[1024,1024]{1,0:T(8,128)(2,1)S(1)}, bf16[1024,1024]{1,0:T(8,128)(2,1)}, u32[]{:S(2)}) %copy-start.3) | copy-done | bytes 2097176
  92.5 0.0 copy-start.4
  92.5 0.0 copy-start.5
  92.5 3.0 %shard_map.50.total_ref = f32[1024,1024]{1,0:T(8,128)S(1)} custom-call(s32[4]{0:T(128)S(1)} %copy-done.6, bf16[1024,1024]{1,0:T(8,128)(2,1)S(1)} %bitcast.10, bf16[1024,1024]{1,0:T(8,128)(2,1)S(1)} %copy-done.3), custom_call_target="tpu_custom_call" | custom-call | flops 2147483648 | bytes 8388608 | tf_op jit(solution)/shard_map/pallas_call | solution.py:177
  95.5 0.0 collective-permute-done.13.rows_ref
  95.5 0.0 copy-done.1
  95.5 0.0 copy-done.4
  95.5 0.0 copy-done.5
  95.5 5.2 %shard_map.51 = bf16[1024,2,512]{2,1,0:T(2,128)(2,1)} custom-call(s32[4]{0:T(128)S(1)} %copy-done.6, bf16[1024,1024]{1,0:T(8,128)(2,1)S(1)} %collective-permute-done.13.rows_ref, bf16[1024,1024]{1,0:T(8,128)(2,1)S(1)} %copy-done.1, f32[1024,1024]{1,0:T(8,128)S(1)} %shard_map.50.total_ref, f32[1,1024]{1,0:T(1,128)S(1)} %get-tuple-element.26.col_len_ref, ...), custom_call_target="tpu_custom_call" | custom-call | flops 2147483648 | bytes 8388608 | tf_op jit(solution)/shard_map/pallas_call | solution.py:223
  (1 shorter events, 0.0 us)
Async XLA Ops:
  22.7 66.2 %all-to-all-start.1 = ((bf16[8,128,1024]{2,0,1:T(8,128)(2,1)}), bf16[8,128,1024]{2,0,1:T(8,128)(2,1)S(1)}, u32[]{:S(2)}, u32[]{:S(2)}) async-start(bf16[8,128,1024]{2,0,1:T(8,128)(2,1)} %bitcast.12), calls=%async_computation.1 | async-start | bytes 4194304 | tf_op jit(solution)/shard_map/all_to_all | solution.py:245
  33.2 11.6 %collective-permute-start = (bf16[64,2176]{1,0:T(8,128)(2,1)S(1)}, bf16[64,2176]{1,0:T(8,128)(2,1)S(1)}, u32[]{:S(2)}, u32[]{:S(2)}) collective-permute-start(bf16[64,2176]{1,0:T(8,128)(2,1)S(1)} %shard_map.47.a_ref), channel_id=1, source_target_pairs={{0,16},{1,65},{2,18},{3,67},{4,20},{5,69},{6,22},{7,71},{8,24},{9,... | collective-permute-start | bytes 835592 | tf_op jit(solution)/shard_map/ppermute | solution.py:44
  34.0 17.6 %collective-permute-start.1 = (bf16[64,2176]{1,0:T(8,128)(2,1)S(1)}, bf16[64,2176]{1,0:T(8,128)(2,1)S(1)}, u32[]{:S(2)}, u32[]{:S(2)}) collective-permute-start(bf16[64,2176]{1,0:T(8,128)(2,1)S(1)} %shard_map.47.a_ref), channel_id=1, source_target_pairs={{0,32},{1,129},{2,34},{3,131},{4,36},{5,133},{6,38},{7,135},{8,40}... | collective-permute-start | bytes 835592 | tf_op jit(solution)/shard_map/ppermute | solution.py:44
  36.8 14.7 %collective-permute-start.2 = (bf16[64,2176]{1,0:T(8,128)(2,1)S(1)}, bf16[64,2176]{1,0:T(8,128)(2,1)S(1)}, u32[]{:S(2)}, u32[]{:S(2)}) collective-permute-start(bf16[64,2176]{1,0:T(8,128)(2,1)S(1)} %shard_map.47.a_ref), channel_id=1, source_target_pairs={{0,48},{1,193},{2,50},{3,195},{4,52},{5,197},{6,54},{7,199},{8,56}... | collective-permute-start | bytes 835592 | tf_op jit(solution)/shard_map/ppermute | solution.py:44
  51.7 13.4 %collective-permute-start.9 = (bf16[256,1024]{1,0:T(8,128)(2,1)S(1)}, bf16[256,1024]{1,0:T(8,128)(2,1)S(1)}, u32[]{:S(2)}, u32[]{:S(2)}) collective-permute-start(bf16[256,1024]{1,0:T(8,128)(2,1)S(1)} %get-tuple-element.19), channel_id=1, source_target_pairs={{0,192},{1,49},{2,194},{3,51},{4,196},{5,53},{6,198},{7,55},{8,200... | collective-permute-start | bytes 1572872 | tf_op jit(solution)/shard_map/ppermute | solution.py:44
  53.2 37.7 %copy-start.6 = (s32[4]{0:T(128)S(1)}, s32[4]{0:T(128)}, u32[]{:S(2)}) copy-start(s32[4]{0:T(128)} %pad_add_fusion.place_ref.at_ref) | copy-start | bytes 52
  53.2 14.6 %collective-permute-start.3 = (bf16[272,1024]{1,0:T(8,128)(2,1)S(1)}, bf16[272,1024]{1,0:T(8,128)(2,1)S(1)}, u32[]{:S(2)}, u32[]{:S(2)}) collective-permute-start(bf16[272,1024]{1,0:T(8,128)(2,1)S(1)} %get-tuple-element.18.refs_0_), channel_id=1, source_target_pairs={{0,64},{1,17},{2,66},{3,19},{4,68},{5,21},{6,70},{7,23},{8,72},{9,... | collective-permute-start | bytes 1671176 | tf_op jit(solution)/shard_map/ppermute | solution.py:44
  53.5 24.4 %collective-permute-start.7 = (bf16[256,1024]{1,0:T(8,128)(2,1)S(1)}, bf16[256,1024]{1,0:T(8,128)(2,1)S(1)}, u32[]{:S(2)}, u32[]{:S(2)}) collective-permute-start(bf16[256,1024]{1,0:T(8,128)(2,1)S(1)} %get-tuple-element.19), channel_id=1, source_target_pairs={{0,64},{1,17},{2,66},{3,19},{4,68},{5,21},{6,70},{7,23},{8,72},{9,... | collective-permute-start | bytes 1572872 | tf_op jit(solution)/shard_map/ppermute | solution.py:44
  54.8 25.4 %collective-permute-start.6 = (bf16[256,1024]{1,0:T(8,128)(2,1)S(1)}, bf16[256,1024]{1,0:T(8,128)(2,1)S(1)}, u32[]{:S(2)}, u32[]{:S(2)}) collective-permute-start(bf16[256,1024]{1,0:T(8,128)(2,1)S(1)} %get-tuple-element.19), channel_id=1, source_target_pairs={{0,1},{1,0},{2,3},{3,2},{4,5},{5,4},{6,7},{7,6},{8,9},{9,8},{10,11... | collective-permute-start | bytes 1572872 | tf_op jit(solution)/shard_map/ppermute | solution.py:48
  65.0 15.2 %collective-permute-start.10 = (bf16[256,1024]{1,0:T(8,128)(2,1)S(1)}, bf16[256,1024]{1,0:T(8,128)(2,1)S(1)}, u32[]{:S(2)}, u32[]{:S(2)}) collective-permute-start(bf16[256,1024]{1,0:T(8,128)(2,1)S(1)} %collective-permute-done.9), channel_id=1, source_target_pairs={{0,192},{1,49},{2,194},{3,51},{4,196},{5,53},{6,198},{7,55},{8,200... | collective-permute-start | bytes 1572872 | tf_op jit(solution)/shard_map/ppermute | solution.py:44
  67.0 18.0 %collective-permute-start.5 = (bf16[272,1024]{1,0:T(8,128)(2,1)S(1)}, bf16[272,1024]{1,0:T(8,128)(2,1)S(1)}, u32[]{:S(2)}, u32[]{:S(2)}) collective-permute-start(bf16[272,1024]{1,0:T(8,128)(2,1)S(1)} %get-tuple-element.18.refs_0_), channel_id=1, source_target_pairs={{0,192},{1,49},{2,194},{3,51},{4,196},{5,53},{6,198},{7,55},{8,200... | collective-permute-start | bytes 1671176 | tf_op jit(solution)/shard_map/ppermute | solution.py:44
  67.8 18.1 %collective-permute-start.4 = (bf16[272,1024]{1,0:T(8,128)(2,1)S(1)}, bf16[272,1024]{1,0:T(8,128)(2,1)S(1)}, u32[]{:S(2)}, u32[]{:S(2)}) collective-permute-start(bf16[272,1024]{1,0:T(8,128)(2,1)S(1)} %collective-permute-done.3.refs_1_), channel_id=1, source_target_pairs={{0,64},{1,17},{2,66},{3,19},{4,68},{5,21},{6,70},{7,23},{8,72},{9,... | collective-permute-start | bytes 1671176 | tf_op jit(solution)/shard_map/ppermute | solution.py:44
  77.9 7.1 %collective-permute-start.12 = (bf16[256,1024]{1,0:T(8,128)(2,1)S(1)}, bf16[256,1024]{1,0:T(8,128)(2,1)S(1)}, u32[]{:S(2)}, u32[]{:S(2)}) collective-permute-start(bf16[256,1024]{1,0:T(8,128)(2,1)S(1)} %collective-permute-done.9), channel_id=1, source_target_pairs={{0,1},{1,0},{2,3},{3,2},{4,5},{5,4},{6,7},{7,6},{8,9},{9,8},{10,11... | collective-permute-start | bytes 1572872 | tf_op jit(solution)/shard_map/ppermute | solution.py:48
  80.2 4.8 %collective-permute-start.8 = (bf16[256,1024]{1,0:T(8,128)(2,1)S(1)}, bf16[256,1024]{1,0:T(8,128)(2,1)S(1)}, u32[]{:S(2)}, u32[]{:S(2)}) collective-permute-start(bf16[256,1024]{1,0:T(8,128)(2,1)S(1)} %collective-permute-done.7), channel_id=1, source_target_pairs={{0,1},{1,0},{2,3},{3,2},{4,5},{5,4},{6,7},{7,6},{8,9},{9,8},{10,11... | collective-permute-start | bytes 1572872 | tf_op jit(solution)/shard_map/ppermute | solution.py:48
  80.2 5.7 %collective-permute-start.11 = (bf16[256,1024]{1,0:T(8,128)(2,1)S(1)}, bf16[256,1024]{1,0:T(8,128)(2,1)S(1)}, u32[]{:S(2)}, u32[]{:S(2)}) collective-permute-start(bf16[256,1024]{1,0:T(8,128)(2,1)S(1)} %collective-permute-done.10), channel_id=1, source_target_pairs={{0,1},{1,0},{2,3},{3,2},{4,5},{5,4},{6,7},{7,6},{8,9},{9,8},{10,11... | collective-permute-start | bytes 1572872 | tf_op jit(solution)/shard_map/ppermute | solution.py:48
  86.2 1.3 %copy-start = (bf16[1024,1024]{1,0:T(8,128)(2,1)}, bf16[1024,1024]{1,0:T(8,128)(2,1)S(1)}, u32[]{:S(2)}) copy-start(bf16[1024,1024]{1,0:T(8,128)(2,1)S(1)} %get-tuple-element.24.panel_ref) | copy-start | bytes 6291460
  87.6 1.3 %copy-start.2 = (bf16[1024,1024]{1,0:T(8,128)(2,1)}, bf16[1024,1024]{1,0:T(8,128)(2,1)S(1)}, u32[]{:S(2)}) copy-start(bf16[1024,1024]{1,0:T(8,128)(2,1)S(1)} %get-tuple-element.25.panel_ref) | copy-start | bytes 6291460
  88.9 6.6 %copy-start.1 = (bf16[1024,1024]{1,0:T(8,128)(2,1)S(1)}, bf16[1024,1024]{1,0:T(8,128)(2,1)}, u32[]{:S(2)}) copy-start(bf16[1024,1024]{1,0:T(8,128)(2,1)} %copy-done) | copy-start | bytes 6291460
  88.9 6.6 %collective-permute-start.13 = (bf16[1024,1024]{1,0:T(8,128)(2,1)S(1)}, bf16[1024,1024]{1,0:T(8,128)(2,1)S(1)}, u32[]{:S(2)}, u32[]{:S(2)}) collective-permute-start(bf16[1024,1024]{1,0:T(8,128)(2,1)S(1)} %bitcast.9), channel_id=1, source_target_pairs={{0,1},{1,0},{2,3},{3,2},{4,5},{5,4},{6,7},{7,6},{8,9},{9,8},{10,11... | collective-permute-start | bytes 6291464 | tf_op jit(solution)/shard_map/ppermute | solution.py:48
  90.9 1.6 %copy-start.3 = (bf16[1024,1024]{1,0:T(8,128)(2,1)S(1)}, bf16[1024,1024]{1,0:T(8,128)(2,1)}, u32[]{:S(2)}) copy-start(bf16[1024,1024]{1,0:T(8,128)(2,1)} %copy-done.2) | copy-start | bytes 6291460
  92.5 3.0 %copy-start.4 = (s32[1024]{0:T(1024)S(1)}, s32[1024]{0:T(1024)}, u32[]{:S(2)}) copy-start(s32[1024]{0:T(1024)} %len_ref.1) | copy-start | bytes 12292
  92.5 3.0 %copy-start.5 = (s32[2,8,8]{2,1,0:T(8,128)S(1)}, s32[2,8,8]{2,1,0:T(8,128)}, u32[]{:S(2)}) copy-start(s32[2,8,8]{2,1,0:T(8,128)} %mask_ref.1) | copy-start | bytes 1540

commit v2 on v1

--- a/solution.py
+++ b/solution.py
@@ -134,9 +134,11 @@
 
 
 def pack_kernel(*refs):
-    panels, swapped, (own_ref, other_ref, len_ref) = refs[:4], refs[4:8], refs[8:]
+    panels, swapped, (near_ref, rest_ref, other_ref, len_ref) = refs[:4], refs[4:8], refs[8:]
+    for i in range(2):
+        near_ref[i * GROUP : (i + 1) * GROUP] = panels[i][:GROUP]
+        rest_ref[i * GROUP : (i + 1) * GROUP] = panels[2 + i][:GROUP]
     for i in range(4):
-        own_ref[i * GROUP : (i + 1) * GROUP] = panels[i][:GROUP]
         other_ref[i * GROUP : (i + 1) * GROUP] = swapped[i][...]
     lens = sum(ref[GROUP:, :BLK].astype(jnp.float32) for ref in panels)
     lens = lens[:8] * 256 + lens[8:]
@@ -144,17 +146,21 @@
 
 
 def pack(panels, swapped):
-    whole = jax.ShapeDtypeStruct((4 * GROUP, WIDTH), jnp.bfloat16)
     return pl.pallas_call(
         pack_kernel,
         in_specs=[VMEM] * 8,
-        out_specs=[VMEM] * 3,
-        out_shape=[whole, whole, jax.ShapeDtypeStruct((1, WIDTH), jnp.float32)],
+        out_specs=[VMEM] * 4,
+        out_shape=[
+            jax.ShapeDtypeStruct((2 * GROUP, WIDTH), jnp.bfloat16),
+            jax.ShapeDtypeStruct((2 * GROUP, WIDTH), jnp.bfloat16),
+            jax.ShapeDtypeStruct((4 * GROUP, WIDTH), jnp.bfloat16),
+            jax.ShapeDtypeStruct((1, WIDTH), jnp.float32),
+        ],
         compiler_params=params(6),
     )(*panels, *swapped)
 
 
-def product(at_ref, rows_ref, panel_ref, x_inside, columns):
+def product(at_ref, rows_ref, panels, x_inside, columns):
     y, x = at_ref[2], at_ref[3]
     parts = []
     for outer in range(4):
@@ -164,24 +170,25 @@
             source = jnp.bitwise_and(y - ry, NY - 1) * NX + jnp.bitwise_and(x - rx, NX - 1)
             parts.append(rows_ref[pl.ds(pl.multiple_of(source * RUN, RUN), RUN), columns])
     rows = jnp.concatenate(parts, axis=0)
-    return lax.dot_general(rows, panel_ref[...], CONTRACT, preferred_element_type=jnp.float32)
-
-
-def first_kernel(at_ref, rows_ref, panel_ref, out_ref):
+    panel = panels[0][...] if len(panels) == 1 else jnp.concatenate([p[...] for p in panels], axis=0)
+    return lax.dot_general(rows, panel, CONTRACT, preferred_element_type=jnp.float32)
+
+
+def first_kernel(at_ref, rows_ref, near_ref, rest_ref, out_ref):
     for i in range(PANEL // ROWS):
         columns = slice(i * ROWS, (i + 1) * ROWS)
-        out_ref[columns, :] = product(at_ref, rows_ref, panel_ref, at_ref[1] == 0, columns)
-
-
-def first_dot(place, local, panel):
+        out_ref[columns, :] = product(at_ref, rows_ref, (near_ref, rest_ref), at_ref[1] == 0, columns)
+
+
+def first_dot(place, local, near, rest):
     return pl.pallas_call(
         first_kernel,
-        in_specs=[SMEM] + [VMEM] * 2,
+        in_specs=[SMEM] + [VMEM] * 3,
         out_specs=VMEM,
         out_shape=jax.ShapeDtypeStruct((PANEL, WIDTH), jnp.float32),
         compiler_params=params(20),
         cost_estimate=pl.CostEstimate(flops=2 << 30, bytes_accessed=8 << 20, transcendentals=0),
-    )(place, local, panel)
+    )(place, local, near, rest)
 
 
 def second_kernel(
@@ -201,7 +208,7 @@
     copies = []
     for i in range(PANEL // ROWS):
         columns = slice(i * ROWS, (i + 1) * ROWS)
-        raw = product(at_ref, rows_ref, panel_ref, at_ref[1] == 1, columns) + total_ref[columns, :]
+        raw = product(at_ref, rows_ref, (panel_ref,), at_ref[1] == 1, columns) + total_ref[columns, :]
         for h in range(ROWS // BLK):
             b = i * (ROWS // BLK) + h
             norm = SCALE * lax.rsqrt(row_lens[:, b : b + 1] * col_len)
@@ -251,10 +258,10 @@
     mine_far, other_far = shift(mine_up, 1, 1), shift(other_down, 1, -1)
     panels = [mine, mine_up, mine_far, mine_down]
     swapped = [swap(a) for a in (other, other_up, other_far, other_down)]
-    own_panel, other_panel, col_len = pack(panels, swapped)
-    local, own_panel, other_panel, col_len = lax.optimization_barrier((local, own_panel, other_panel, col_len))
+    near, rest, other_panel, col_len = pack(panels, swapped)
+    local, near, rest, other_panel, col_len = lax.optimization_barrier((local, near, rest, other_panel, col_len))
     remote = swap(local)
-    total = first_dot(place, local, own_panel)
+    total = first_dot(place, local, near, rest)
     return second_dot(place, remote, other_panel, total, col_len, lengths.reshape(PANEL // BLK, BLK), block_mask)
 
 

time: 101 us -> 100 us (0.990)
  no operation moved by 1% of the time
where the time goes in v2:
time: 100 us
  waiting for transfers between devices  38.2 us (38%)
  starting transfers between devices  26.9 us (27%)
  blocking collectives  19.9 us (20%)
  Pallas kernels  10.7 us (11%)
  local copies, waits for them, and re-layouts  3.54 us (4%)
    ppermute x9, waiting for transfers between devices, shift(): return lax.ppermute(value, ('seq', 'kmer'), pairs)  38.2 us
    all_to_all x1, blocking collectives, shards(): lax.all_to_all(piece, 'seq', 0, 0, axis_index_groups=LINES, tiled=True)  19.9 us
    ppermute x9, starting transfers between devices, shift(): return lax.ppermute(value, ('seq', 'kmer'), pairs)  11.2 us
    all_to_all x1, starting transfers between devices, shards(): lax.all_to_all(profiles, 'seq', split_axis=1, concat_axis=0, tiled=True)  10.5 us
    ppermute x5, starting transfers between devices, swap(): return lax.ppermute(value, 'kmer', SWAP)  5.2 us
    pallas_call x1, Pallas kernels, second_dot(): pl.pallas_call(second_kernel, in_specs=[SMEM] + [VMEM] * 6, out_specs=pl....  5.15 us
    unnamed x14, local copies, waits for them, and re-layouts  3.54 us
    pallas_call x1, Pallas kernels, first_dot(): pl.pallas_call(first_kernel, in_specs=[SMEM] + [VMEM] * 3, out_specs=VMEM...  2.95 us
  transfers between devices with their start and end apart: 15, of which 6 were waited for; matrix products, arithmetic and copies ran while one was open for 0% of the time, Pallas kernels for 3%

profile of v2, /device:TPU:1, one launch (start us, length us, event | category | flops | bytes accessed | tf_op | source)
XLA Modules:
  0.0 100.1 jit_solution(10849359867203972330)
XLA Ops:
  0.0 0.7 pad_add_fusion.place_ref.at_ref
  0.7 2.2 %shard_map.46 = bf16[8,8,2304]{2,1,0:T(8,128)(2,1)} custom-call(s32[2]{0:T(128)} %own_ref.1, s32[4]{0:T(128)} %pad_add_fusion.place_ref.at_ref, bf16[8,131072]{1,0:T(8,128)(2,1)} %d_ref.1, bf16[8,131072]{1,0:T(8,128)(2,1)} %d_ref.1, bf16[8,131072]{1,0:T(8,128)(2,1)} %d_ref.1, bf16[8,131072]{1,0:T(8,128)(2,1)} %d_ref.1, s32[1024]{0:T(1024)} %len_ref.1), custom_call_target="tpu_custom_call" | custom-call | tf_op jit(solution)/shard_map/pallas_call | solution.py:76
  2.8 19.9 %all_to_all.24.line_ref = bf16[8,8,2304]{2,1,0:T(8,128)(2,1)S(1)} all-to-all(bf16[8,8,2304]{2,1,0:T(8,128)(2,1)} %shard_map.46), channel_id=1, replica_groups={{0,2,4,6,8,10,12,14},{16,18,20,22,24,26,28,30},{32,34,36,38,40,42,44,46..., dimensions={0} | all-to-all | bytes 589824 | tf_op jit(solution)/shard_map/all_to_all | solution.py:250
  22.7 10.5 %all-to-all-start.1 = ((bf16[8,128,1024]{2,0,1:T(8,128)(2,1)}), bf16[8,128,1024]{2,0,1:T(8,128)(2,1)S(1)}, u32[]{:S(2)}, u32[]{:S(2)}) async-start(bf16[8,128,1024]{2,0,1:T(8,128)(2,1)} %bitcast.12), calls=%async_computation.1 | async-start | bytes 4194304 | tf_op jit(solution)/shard_map/all_to_all | solution.py:252
  33.2 0.8 collective-permute-start
  34.0 2.8 %collective-permute-start.1 = (bf16[64,2176]{1,0:T(8,128)(2,1)S(1)}, bf16[64,2176]{1,0:T(8,128)(2,1)S(1)}, u32[]{:S(2)}, u32[]{:S(2)}) collective-permute-start(bf16[64,2176]{1,0:T(8,128)(2,1)S(1)} %shard_map.47.a_ref), channel_id=1, source_target_pairs={{0,32},{1,129},{2,34},{3,131},{4,36},{5,133},{6,38},{7,135},{8,40}... | collective-permute-start | bytes 835592 | tf_op jit(solution)/shard_map/ppermute | solution.py:44
  36.8 1.0 collective-permute-start.2
  37.8 7.1 %collective-permute-done.b_ref = bf16[64,2176]{1,0:T(8,128)(2,1)S(1)} collective-permute-done((bf16[64,2176]{1,0:T(8,128)(2,1)S(1)}, bf16[64,2176]{1,0:T(8,128)(2,1)S(1)}, u32[]{:S(2)}, u32[]{:S(2)}) %collective-permute-start) | collective-permute-done | bytes 278560 | tf_op jit(solution)/shard_map/ppermute | solution.py:44
  44.8 6.7 %collective-permute-done.1.c_ref = bf16[64,2176]{1,0:T(8,128)(2,1)S(1)} collective-permute-done((bf16[64,2176]{1,0:T(8,128)(2,1)S(1)}, bf16[64,2176]{1,0:T(8,128)(2,1)S(1)}, u32[]{:S(2)}, u32[]{:S(2)}) %collective-permute-start.1) | collective-permute-done | bytes 278560 | tf_op jit(solution)/shard_map/ppermute | solution.py:44
  51.5 0.0 collective-permute-done.2.d_ref
  51.6 0.1 shard_map.48
  51.6 1.6 %collective-permute-start.9 = (bf16[256,1024]{1,0:T(8,128)(2,1)S(1)}, bf16[256,1024]{1,0:T(8,128)(2,1)S(1)}, u32[]{:S(2)}, u32[]{:S(2)}) collective-permute-start(bf16[256,1024]{1,0:T(8,128)(2,1)S(1)} %get-tuple-element.21), channel_id=1, source_target_pairs={{0,192},{1,49},{2,194},{3,51},{4,196},{5,53},{6,198},{7,55},{8,200... | collective-permute-start | bytes 1572872 | tf_op jit(solution)/shard_map/ppermute | solution.py:44
  53.2 0.0 copy-start.6
  53.2 0.2 collective-permute-start.3
  53.5 1.4 %collective-permute-start.7 = (bf16[256,1024]{1,0:T(8,128)(2,1)S(1)}, bf16[256,1024]{1,0:T(8,128)(2,1)S(1)}, u32[]{:S(2)}, u32[]{:S(2)}) collective-permute-start(bf16[256,1024]{1,0:T(8,128)(2,1)S(1)} %get-tuple-element.21), channel_id=1, source_target_pairs={{0,64},{1,17},{2,66},{3,19},{4,68},{5,21},{6,70},{7,23},{8,72},{9,... | collective-permute-start | bytes 1572872 | tf_op jit(solution)/shard_map/ppermute | solution.py:44
  54.8 0.3 collective-permute-start.6
  55.2 9.8 %collective-permute-done.9 = bf16[256,1024]{1,0:T(8,128)(2,1)S(1)} collective-permute-done((bf16[256,1024]{1,0:T(8,128)(2,1)S(1)}, bf16[256,1024]{1,0:T(8,128)(2,1)S(1)}, u32[]{:S(2)}, u32[]{:S(2)}) %collective-permute-start.9) | collective-permute-done | bytes 524320 | tf_op jit(solution)/shard_map/ppermute | solution.py:44
  65.0 2.0 %collective-permute-start.10 = (bf16[256,1024]{1,0:T(8,128)(2,1)S(1)}, bf16[256,1024]{1,0:T(8,128)(2,1)S(1)}, u32[]{:S(2)}, u32[]{:S(2)}) collective-permute-start(bf16[256,1024]{1,0:T(8,128)(2,1)S(1)} %collective-permute-done.9), channel_id=1, source_target_pairs={{0,192},{1,49},{2,194},{3,51},{4,196},{5,53},{6,198},{7,55},{8,200... | collective-permute-start | bytes 1572872 | tf_op jit(solution)/shard_map/ppermute | solution.py:44
  67.0 0.8 collective-permute-start.5
  67.8 0.0 collective-permute-done.3.refs_1_
  67.8 0.6 collective-permute-start.4
  68.4 9.4 %collective-permute-done.7 = bf16[256,1024]{1,0:T(8,128)(2,1)S(1)} collective-permute-done((bf16[256,1024]{1,0:T(8,128)(2,1)S(1)}, bf16[256,1024]{1,0:T(8,128)(2,1)S(1)}, u32[]{:S(2)}, u32[]{:S(2)}) %collective-permute-start.7) | collective-permute-done | bytes 524320 | tf_op jit(solution)/shard_map/ppermute | solution.py:44
  77.8 2.4 %collective-permute-start.12 = (bf16[256,1024]{1,0:T(8,128)(2,1)S(1)}, bf16[256,1024]{1,0:T(8,128)(2,1)S(1)}, u32[]{:S(2)}, u32[]{:S(2)}) collective-permute-start(bf16[256,1024]{1,0:T(8,128)(2,1)S(1)} %collective-permute-done.9), channel_id=1, source_target_pairs={{0,1},{1,0},{2,3},{3,2},{4,5},{5,4},{6,7},{7,6},{8,9},{9,8},{10,11... | collective-permute-start | bytes 1572872 | tf_op jit(solution)/shard_map/ppermute | solution.py:48
  80.2 0.0 collective-permute-done.6.refs_4_
  80.2 0.0 collective-permute-start.8
  80.2 0.0 collective-permute-done.10
  80.2 0.5 collective-permute-start.11
  80.7 4.2 %collective-permute-done.5.refs_3_ = bf16[272,1024]{1,0:T(8,128)(2,1)S(1)} collective-permute-done((bf16[272,1024]{1,0:T(8,128)(2,1)S(1)}, bf16[272,1024]{1,0:T(8,128)(2,1)S(1)}, u32[]{:S(2)}, u32[]{:S(2)}) %collective-permute-start.5) | collective-permute-done | bytes 557088 | tf_op jit(solution)/shard_map/ppermute | solution.py:44
  85.0 0.0 collective-permute-done.12.refs_7_
  85.0 0.0 collective-permute-done.8.refs_5_
  85.0 1.0 collective-permute-done.4.refs_2_
  85.9 0.0 collective-permute-done.11.refs_6_
  85.9 0.3 shard_map.49
  86.2 0.0 copy-start
  86.2 1.3 %copy-done = bf16[1024,1024]{1,0:T(8,128)(2,1)} copy-done((bf16[1024,1024]{1,0:T(8,128)(2,1)}, bf16[1024,1024]{1,0:T(8,128)(2,1)S(1)}, u32[]{:S(2)}) %copy-start) | copy-done | bytes 2097176
  87.5 0.0 copy-start.2
  87.5 1.0 copy-done.2
  88.5 0.0 all-to-all-done.1
  88.5 0.0 copy-start.1
  88.5 2.0 %collective-permute-start.13 = (bf16[1024,1024]{1,0:T(8,128)(2,1)S(1)}, bf16[1024,1024]{1,0:T(8,128)(2,1)S(1)}, u32[]{:S(2)}, u32[]{:S(2)}) collective-permute-start(bf16[1024,1024]{1,0:T(8,128)(2,1)S(1)} %bitcast.9), channel_id=1, source_target_pairs={{0,1},{1,0},{2,3},{3,2},{4,5},{5,4},{6,7},{7,6},{8,9},{9,8},{10,11... | collective-permute-start | bytes 6291464 | tf_op jit(solution)/shard_map/ppermute | solution.py:48
  90.5 0.0 copy-done.6
  90.5 0.0 copy-start.3
  90.5 1.2 %copy-done.3 = bf16[512,1024]{1,0:T(8,128)(2,1)S(1)} copy-done((bf16[512,1024]{1,0:T(8,128)(2,1)S(1)}, bf16[512,1024]{1,0:T(8,128)(2,1)}, u32[]{:S(2)}) %copy-start.3) | copy-done | bytes 1048600
  91.8 0.0 copy-start.4
  91.8 0.0 copy-start.5
  91.8 3.0 %shard_map.50.total_ref = f32[1024,1024]{1,0:T(8,128)S(1)} custom-call(s32[4]{0:T(128)S(1)} %copy-done.6, bf16[1024,1024]{1,0:T(8,128)(2,1)S(1)} %bitcast.10, bf16[512,1024]{1,0:T(8,128)(2,1)S(1)} %get-tuple-element.28.near_ref, bf16[512,1024]{1,0:T(8,128)(2,1)S(1)} %copy-done.3), custom_call_target="tpu_custom_call" | custom-call | flops 2147483648 | bytes 8388608 | tf_op jit(solution)/shard_map/pallas_call | solution.py:184
  94.7 0.0 collective-permute-done.13.rows_ref
  94.7 0.0 copy-done.1
  94.7 0.0 copy-done.4
  94.7 0.0 copy-done.5
  94.8 5.1 %shard_map.51 = bf16[1024,2,512]{2,1,0:T(2,128)(2,1)} custom-call(s32[4]{0:T(128)S(1)} %copy-done.6, bf16[1024,1024]{1,0:T(8,128)(2,1)S(1)} %collective-permute-done.13.rows_ref, bf16[1024,1024]{1,0:T(8,128)(2,1)S(1)} %copy-done.1, f32[1024,1024]{1,0:T(8,128)S(1)} %shard_map.50.total_ref, f32[1,1024]{1,0:T(1,128)S(1)} %get-tuple-element.30.col_len_ref, ...), custom_call_target="tpu_custom_call" | custom-call | flops 2147483648 | bytes 8388608 | tf_op jit(solution)/shard_map/pallas_call | solution.py:230
  (1 shorter events, 0.0 us)
Async XLA Ops:
  22.7 65.9 %all-to-all-start.1 = ((bf16[8,128,1024]{2,0,1:T(8,128)(2,1)}), bf16[8,128,1024]{2,0,1:T(8,128)(2,1)S(1)}, u32[]{:S(2)}, u32[]{:S(2)}) async-start(bf16[8,128,1024]{2,0,1:T(8,128)(2,1)} %bitcast.12), calls=%async_computation.1 | async-start | bytes 4194304 | tf_op jit(solution)/shard_map/all_to_all | solution.py:252
  33.2 11.6 %collective-permute-start = (bf16[64,2176]{1,0:T(8,128)(2,1)S(1)}, bf16[64,2176]{1,0:T(8,128)(2,1)S(1)}, u32[]{:S(2)}, u32[]{:S(2)}) collective-permute-start(bf16[64,2176]{1,0:T(8,128)(2,1)S(1)} %shard_map.47.a_ref), channel_id=1, source_target_pairs={{0,16},{1,65},{2,18},{3,67},{4,20},{5,69},{6,22},{7,71},{8,24},{9,... | collective-permute-start | bytes 835592 | tf_op jit(solution)/shard_map/ppermute | solution.py:44
  34.0 17.6 %collective-permute-start.1 = (bf16[64,2176]{1,0:T(8,128)(2,1)S(1)}, bf16[64,2176]{1,0:T(8,128)(2,1)S(1)}, u32[]{:S(2)}, u32[]{:S(2)}) collective-permute-start(bf16[64,2176]{1,0:T(8,128)(2,1)S(1)} %shard_map.47.a_ref), channel_id=1, source_target_pairs={{0,32},{1,129},{2,34},{3,131},{4,36},{5,133},{6,38},{7,135},{8,40}... | collective-permute-start | bytes 835592 | tf_op jit(solution)/shard_map/ppermute | solution.py:44
  36.8 14.7 %collective-permute-start.2 = (bf16[64,2176]{1,0:T(8,128)(2,1)S(1)}, bf16[64,2176]{1,0:T(8,128)(2,1)S(1)}, u32[]{:S(2)}, u32[]{:S(2)}) collective-permute-start(bf16[64,2176]{1,0:T(8,128)(2,1)S(1)} %shard_map.47.a_ref), channel_id=1, source_target_pairs={{0,48},{1,193},{2,50},{3,195},{4,52},{5,197},{6,54},{7,199},{8,56}... | collective-permute-start | bytes 835592 | tf_op jit(solution)/shard_map/ppermute | solution.py:44
  51.6 13.4 %collective-permute-start.9 = (bf16[256,1024]{1,0:T(8,128)(2,1)S(1)}, bf16[256,1024]{1,0:T(8,128)(2,1)S(1)}, u32[]{:S(2)}, u32[]{:S(2)}) collective-permute-start(bf16[256,1024]{1,0:T(8,128)(2,1)S(1)} %get-tuple-element.21), channel_id=1, source_target_pairs={{0,192},{1,49},{2,194},{3,51},{4,196},{5,53},{6,198},{7,55},{8,200... | collective-permute-start | bytes 1572872 | tf_op jit(solution)/shard_map/ppermute | solution.py:44
  53.2 37.3 %copy-start.6 = (s32[4]{0:T(128)S(1)}, s32[4]{0:T(128)}, u32[]{:S(2)}) copy-start(s32[4]{0:T(128)} %pad_add_fusion.place_ref.at_ref) | copy-start | bytes 52
  53.2 14.6 %collective-permute-start.3 = (bf16[272,1024]{1,0:T(8,128)(2,1)S(1)}, bf16[272,1024]{1,0:T(8,128)(2,1)S(1)}, u32[]{:S(2)}, u32[]{:S(2)}) collective-permute-start(bf16[272,1024]{1,0:T(8,128)(2,1)S(1)} %get-tuple-element.20.refs_0_), channel_id=1, source_target_pairs={{0,64},{1,17},{2,66},{3,19},{4,68},{5,21},{6,70},{7,23},{8,72},{9,... | collective-permute-start | bytes 1671176 | tf_op jit(solution)/shard_map/ppermute | solution.py:44
  53.5 24.4 %collective-permute-start.7 = (bf16[256,1024]{1,0:T(8,128)(2,1)S(1)}, bf16[256,1024]{1,0:T(8,128)(2,1)S(1)}, u32[]{:S(2)}, u32[]{:S(2)}) collective-permute-start(bf16[256,1024]{1,0:T(8,128)(2,1)S(1)} %get-tuple-element.21), channel_id=1, source_target_pairs={{0,64},{1,17},{2,66},{3,19},{4,68},{5,21},{6,70},{7,23},{8,72},{9,... | collective-permute-start | bytes 1572872 | tf_op jit(solution)/shard_map/ppermute | solution.py:44
  54.8 25.4 %collective-permute-start.6 = (bf16[256,1024]{1,0:T(8,128)(2,1)S(1)}, bf16[256,1024]{1,0:T(8,128)(2,1)S(1)}, u32[]{:S(2)}, u32[]{:S(2)}) collective-permute-start(bf16[256,1024]{1,0:T(8,128)(2,1)S(1)} %get-tuple-element.21), channel_id=1, source_target_pairs={{0,1},{1,0},{2,3},{3,2},{4,5},{5,4},{6,7},{7,6},{8,9},{9,8},{10,11... | collective-permute-start | bytes 1572872 | tf_op jit(solution)/shard_map/ppermute | solution.py:48
  65.0 15.2 %collective-permute-start.10 = (bf16[256,1024]{1,0:T(8,128)(2,1)S(1)}, bf16[256,1024]{1,0:T(8,128)(2,1)S(1)}, u32[]{:S(2)}, u32[]{:S(2)}) collective-permute-start(bf16[256,1024]{1,0:T(8,128)(2,1)S(1)} %collective-permute-done.9), channel_id=1, source_target_pairs={{0,192},{1,49},{2,194},{3,51},{4,196},{5,53},{6,198},{7,55},{8,200... | collective-permute-start | bytes 1572872 | tf_op jit(solution)/shard_map/ppermute | solution.py:44
  67.0 18.0 %collective-permute-start.5 = (bf16[272,1024]{1,0:T(8,128)(2,1)S(1)}, bf16[272,1024]{1,0:T(8,128)(2,1)S(1)}, u32[]{:S(2)}, u32[]{:S(2)}) collective-permute-start(bf16[272,1024]{1,0:T(8,128)(2,1)S(1)} %get-tuple-element.20.refs_0_), channel_id=1, source_target_pairs={{0,192},{1,49},{2,194},{3,51},{4,196},{5,53},{6,198},{7,55},{8,200... | collective-permute-start | bytes 1671176 | tf_op jit(solution)/shard_map/ppermute | solution.py:44
  67.8 18.1 %collective-permute-start.4 = (bf16[272,1024]{1,0:T(8,128)(2,1)S(1)}, bf16[272,1024]{1,0:T(8,128)(2,1)S(1)}, u32[]{:S(2)}, u32[]{:S(2)}) collective-permute-start(bf16[272,1024]{1,0:T(8,128)(2,1)S(1)} %collective-permute-done.3.refs_1_), channel_id=1, source_target_pairs={{0,64},{1,17},{2,66},{3,19},{4,68},{5,21},{6,70},{7,23},{8,72},{9,... | collective-permute-start | bytes 1671176 | tf_op jit(solution)/shard_map/ppermute | solution.py:44
  77.8 7.1 %collective-permute-start.12 = (bf16[256,1024]{1,0:T(8,128)(2,1)S(1)}, bf16[256,1024]{1,0:T(8,128)(2,1)S(1)}, u32[]{:S(2)}, u32[]{:S(2)}) collective-permute-start(bf16[256,1024]{1,0:T(8,128)(2,1)S(1)} %collective-permute-done.9), channel_id=1, source_target_pairs={{0,1},{1,0},{2,3},{3,2},{4,5},{5,4},{6,7},{7,6},{8,9},{9,8},{10,11... | collective-permute-start | bytes 1572872 | tf_op jit(solution)/shard_map/ppermute | solution.py:48
  80.2 4.8 %collective-permute-start.8 = (bf16[256,1024]{1,0:T(8,128)(2,1)S(1)}, bf16[256,1024]{1,0:T(8,128)(2,1)S(1)}, u32[]{:S(2)}, u32[]{:S(2)}) collective-permute-start(bf16[256,1024]{1,0:T(8,128)(2,1)S(1)} %collective-permute-done.7), channel_id=1, source_target_pairs={{0,1},{1,0},{2,3},{3,2},{4,5},{5,4},{6,7},{7,6},{8,9},{9,8},{10,11... | collective-permute-start | bytes 1572872 | tf_op jit(solution)/shard_map/ppermute | solution.py:48
  80.2 5.7 %collective-permute-start.11 = (bf16[256,1024]{1,0:T(8,128)(2,1)S(1)}, bf16[256,1024]{1,0:T(8,128)(2,1)S(1)}, u32[]{:S(2)}, u32[]{:S(2)}) collective-permute-start(bf16[256,1024]{1,0:T(8,128)(2,1)S(1)} %collective-permute-done.10), channel_id=1, source_target_pairs={{0,1},{1,0},{2,3},{3,2},{4,5},{5,4},{6,7},{7,6},{8,9},{9,8},{10,11... | collective-permute-start | bytes 1572872 | tf_op jit(solution)/shard_map/ppermute | solution.py:48
  86.2 1.3 %copy-start = (bf16[1024,1024]{1,0:T(8,128)(2,1)}, bf16[1024,1024]{1,0:T(8,128)(2,1)S(1)}, u32[]{:S(2)}) copy-start(bf16[1024,1024]{1,0:T(8,128)(2,1)S(1)} %get-tuple-element.27.panel_ref) | copy-start | bytes 6291460
  87.5 1.0 copy-start.2
  88.5 6.2 %copy-start.1 = (bf16[1024,1024]{1,0:T(8,128)(2,1)S(1)}, bf16[1024,1024]{1,0:T(8,128)(2,1)}, u32[]{:S(2)}) copy-start(bf16[1024,1024]{1,0:T(8,128)(2,1)} %copy-done) | copy-start | bytes 6291460
  88.5 6.2 %collective-permute-start.13 = (bf16[1024,1024]{1,0:T(8,128)(2,1)S(1)}, bf16[1024,1024]{1,0:T(8,128)(2,1)S(1)}, u32[]{:S(2)}, u32[]{:S(2)}) collective-permute-start(bf16[1024,1024]{1,0:T(8,128)(2,1)S(1)} %bitcast.9), channel_id=1, source_target_pairs={{0,1},{1,0},{2,3},{3,2},{4,5},{5,4},{6,7},{7,6},{8,9},{9,8},{10,11... | collective-permute-start | bytes 6291464 | tf_op jit(solution)/shard_map/ppermute | solution.py:48
  90.5 1.2 %copy-start.3 = (bf16[512,1024]{1,0:T(8,128)(2,1)S(1)}, bf16[512,1024]{1,0:T(8,128)(2,1)}, u32[]{:S(2)}) copy-start(bf16[512,1024]{1,0:T(8,128)(2,1)} %copy-done.2) | copy-start | bytes 3145732
  91.8 3.0 %copy-start.4 = (s32[1024]{0:T(1024)S(1)}, s32[1024]{0:T(1024)}, u32[]{:S(2)}) copy-start(s32[1024]{0:T(1024)} %len_ref.1) | copy-start | bytes 12292
  91.8 3.0 %copy-start.5 = (s32[2,8,8]{2,1,0:T(8,128)S(1)}, s32[2,8,8]{2,1,0:T(8,128)}, u32[]{:S(2)}) copy-start(s32[2,8,8]{2,1,0:T(8,128)} %mask_ref.1) | copy-start | bytes 1540

commit v3 on v2

--- a/solution.py
+++ b/solution.py
@@ -134,30 +134,41 @@
 
 
 def pack_kernel(*refs):
-    panels, swapped, (near_ref, rest_ref, other_ref, len_ref) = refs[:4], refs[4:8], refs[8:]
+    blocks, out_ref = refs[:-1], refs[-1]
+    for i, ref in enumerate(blocks):
+        out_ref[i * GROUP : (i + 1) * GROUP] = ref[:GROUP]
+
+
+def pack(*blocks):
+    return pl.pallas_call(
+        pack_kernel,
+        in_specs=[VMEM] * len(blocks),
+        out_specs=VMEM,
+        out_shape=jax.ShapeDtypeStruct((len(blocks) * GROUP, WIDTH), jnp.bfloat16),
+        compiler_params=params(6),
+    )(*blocks)
+
+
+def pack_last_kernel(*refs):
+    panels, (rest_ref, len_ref) = refs[:4], refs[4:]
     for i in range(2):
-        near_ref[i * GROUP : (i + 1) * GROUP] = panels[i][:GROUP]
         rest_ref[i * GROUP : (i + 1) * GROUP] = panels[2 + i][:GROUP]
-    for i in range(4):
-        other_ref[i * GROUP : (i + 1) * GROUP] = swapped[i][...]
     lens = sum(ref[GROUP:, :BLK].astype(jnp.float32) for ref in panels)
     lens = lens[:8] * 256 + lens[8:]
     len_ref[...] = jnp.concatenate([lens[j : j + 1] for j in range(8)], axis=1)
 
 
-def pack(panels, swapped):
-    return pl.pallas_call(
-        pack_kernel,
-        in_specs=[VMEM] * 8,
-        out_specs=[VMEM] * 4,
+def pack_last(*panels):
+    return pl.pallas_call(
+        pack_last_kernel,
+        in_specs=[VMEM] * 4,
+        out_specs=[VMEM] * 2,
         out_shape=[
             jax.ShapeDtypeStruct((2 * GROUP, WIDTH), jnp.bfloat16),
-            jax.ShapeDtypeStruct((2 * GROUP, WIDTH), jnp.bfloat16),
-            jax.ShapeDtypeStruct((4 * GROUP, WIDTH), jnp.bfloat16),
             jax.ShapeDtypeStruct((1, WIDTH), jnp.float32),
         ],
         compiler_params=params(6),
-    )(*panels, *swapped)
+    )(*panels)
 
 
 def product(at_ref, rows_ref, panels, x_inside, columns):
@@ -258,7 +269,10 @@
     mine_far, other_far = shift(mine_up, 1, 1), shift(other_down, 1, -1)
     panels = [mine, mine_up, mine_far, mine_down]
     swapped = [swap(a) for a in (other, other_up, other_far, other_down)]
-    near, rest, other_panel, col_len = pack(panels, swapped)
+    near = pack(*panels[:2])
+    other_panel = pack(*swapped)
+    panels[3], other_panel = lax.optimization_barrier((panels[3], other_panel))
+    rest, col_len = pack_last(*panels)
     local, near, rest, other_panel, col_len = lax.optimization_barrier((local, near, rest, other_panel, col_len))
     remote = swap(local)
     total = first_dot(place, local, near, rest)

time: 100 us -> 98.9 us (0.989)
  waiting for transfers between devices: 38.2 us -> 36.7 us
    ppermute x9, waiting for transfers between devices: 38.2 us -> 34.2 us  [shift(): return lax.ppermute(value, ('seq', 'kmer'), pairs)]
    ppermute x5, waiting for transfers between devices: 0.01 us -> 2.45 us  [swap(): return lax.ppermute(value, 'kmer', SWAP)]
  transfers between devices with their start and end apart: 15 -> 15, of which waited for: 6 -> 9; matrix products, arithmetic and copies ran while one was open for 0% -> 0% of each run, Pallas kernels for 3% -> 3%
where the time goes in v3:
time: 98.9 us; the launch traced here: 98.5 us
  waiting for transfers between devices  36.7 us (37%)
  starting transfers between devices  26.9 us (27%)
  blocking collectives  19.9 us (20%)
  Pallas kernels  10.7 us (11%)
  local copies, waits for them, and re-layouts  3.54 us (4%)
    ppermute x9, waiting for transfers between devices, shift(): return lax.ppermute(value, ('seq', 'kmer'), pairs)  34.2 us
    all_to_all x1, blocking collectives, shards(): lax.all_to_all(piece, 'seq', 0, 0, axis_index_groups=LINES, tiled=True)  19.9 us
    ppermute x9, starting transfers between devices, shift(): return lax.ppermute(value, ('seq', 'kmer'), pairs)  11.2 us
    all_to_all x1, starting transfers between devices, shards(): lax.all_to_all(profiles, 'seq', split_axis=1, concat_axis=0, tiled=True)  10.5 us
    ppermute x5, starting transfers between devices, swap(): return lax.ppermute(value, 'kmer', SWAP)  5.21 us
    pallas_call x1, Pallas kernels, second_dot(): pl.pallas_call(second_kernel, in_specs=[SMEM] + [VMEM] * 6, out_specs=pl....  5.15 us
    unnamed x14, local copies, waits for them, and re-layouts  3.54 us
    pallas_call x1, Pallas kernels, first_dot(): pl.pallas_call(first_kernel, in_specs=[SMEM] + [VMEM] * 3, out_specs=VMEM...  2.94 us
  transfers between devices with their start and end apart: 15, of which 9 were waited for; matrix products, arithmetic and copies ran while one was open for 0% of the time, Pallas kernels for 3%

profile of v3, /device:TPU:1, one launch (start us, length us, event | category | flops | bytes accessed | tf_op | source)
XLA Modules:
  0.0 98.5 jit_solution(17805106716217776198)
XLA Ops:
  0.0 0.7 pad_add_fusion.place_ref.at_ref
  0.7 2.2 %shard_map.46 = bf16[8,8,2304]{2,1,0:T(8,128)(2,1)} custom-call(s32[2]{0:T(128)} %own_ref.1, s32[4]{0:T(128)} %pad_add_fusion.place_ref.at_ref, bf16[8,131072]{1,0:T(8,128)(2,1)} %d_ref.1, bf16[8,131072]{1,0:T(8,128)(2,1)} %d_ref.1, bf16[8,131072]{1,0:T(8,128)(2,1)} %d_ref.1, bf16[8,131072]{1,0:T(8,128)(2,1)} %d_ref.1, s32[1024]{0:T(1024)} %len_ref.1), custom_call_target="tpu_custom_call" | custom-call | tf_op jit(solution)/shard_map/pallas_call | solution.py:76
  2.8 19.9 %all_to_all.24.line_ref = bf16[8,8,2304]{2,1,0:T(8,128)(2,1)S(1)} all-to-all(bf16[8,8,2304]{2,1,0:T(8,128)(2,1)} %shard_map.46), channel_id=1, replica_groups={{0,2,4,6,8,10,12,14},{16,18,20,22,24,26,28,30},{32,34,36,38,40,42,44,46..., dimensions={0} | all-to-all | bytes 589824 | tf_op jit(solution)/shard_map/all_to_all | solution.py:261
  22.7 10.5 %all-to-all-start.1 = ((bf16[8,128,1024]{2,0,1:T(8,128)(2,1)}), bf16[8,128,1024]{2,0,1:T(8,128)(2,1)S(1)}, u32[]{:S(2)}, u32[]{:S(2)}) async-start(bf16[8,128,1024]{2,0,1:T(8,128)(2,1)} %bitcast.12), calls=%async_computation.1 | async-start | bytes 4194304 | tf_op jit(solution)/shard_map/all_to_all | solution.py:263
  33.2 0.8 collective-permute-start
  34.0 2.8 %collective-permute-start.1 = (bf16[64,2176]{1,0:T(8,128)(2,1)S(1)}, bf16[64,2176]{1,0:T(8,128)(2,1)S(1)}, u32[]{:S(2)}, u32[]{:S(2)}) collective-permute-start(bf16[64,2176]{1,0:T(8,128)(2,1)S(1)} %shard_map.47.a_ref), channel_id=1, source_target_pairs={{0,32},{1,129},{2,34},{3,131},{4,36},{5,133},{6,38},{7,135},{8,40}... | collective-permute-start | bytes 835592 | tf_op jit(solution)/shard_map/ppermute | solution.py:44
  36.8 1.0 collective-permute-start.2
  37.8 7.1 %collective-permute-done.b_ref = bf16[64,2176]{1,0:T(8,128)(2,1)S(1)} collective-permute-done((bf16[64,2176]{1,0:T(8,128)(2,1)S(1)}, bf16[64,2176]{1,0:T(8,128)(2,1)S(1)}, u32[]{:S(2)}, u32[]{:S(2)}) %collective-permute-start) | collective-permute-done | bytes 278560 | tf_op jit(solution)/shard_map/ppermute | solution.py:44
  44.8 6.7 %collective-permute-done.1.c_ref = bf16[64,2176]{1,0:T(8,128)(2,1)S(1)} collective-permute-done((bf16[64,2176]{1,0:T(8,128)(2,1)S(1)}, bf16[64,2176]{1,0:T(8,128)(2,1)S(1)}, u32[]{:S(2)}, u32[]{:S(2)}) %collective-permute-start.1) | collective-permute-done | bytes 278560 | tf_op jit(solution)/shard_map/ppermute | solution.py:44
  51.5 0.0 collective-permute-done.2.d_ref
  51.6 0.1 shard_map.48
  51.6 1.6 %collective-permute-start.9 = (bf16[256,1024]{1,0:T(8,128)(2,1)S(1)}, bf16[256,1024]{1,0:T(8,128)(2,1)S(1)}, u32[]{:S(2)}, u32[]{:S(2)}) collective-permute-start(bf16[256,1024]{1,0:T(8,128)(2,1)S(1)} %get-tuple-element.21), channel_id=1, source_target_pairs={{0,192},{1,49},{2,194},{3,51},{4,196},{5,53},{6,198},{7,55},{8,200... | collective-permute-start | bytes 1572872 | tf_op jit(solution)/shard_map/ppermute | solution.py:44
  53.2 0.2 collective-permute-start.3
  53.4 1.4 %collective-permute-start.7 = (bf16[256,1024]{1,0:T(8,128)(2,1)S(1)}, bf16[256,1024]{1,0:T(8,128)(2,1)S(1)}, u32[]{:S(2)}, u32[]{:S(2)}) collective-permute-start(bf16[256,1024]{1,0:T(8,128)(2,1)S(1)} %get-tuple-element.21), channel_id=1, source_target_pairs={{0,64},{1,17},{2,66},{3,19},{4,68},{5,21},{6,70},{7,23},{8,72},{9,... | collective-permute-start | bytes 1572872 | tf_op jit(solution)/shard_map/ppermute | solution.py:44
  54.8 0.3 collective-permute-start.6
  55.2 9.8 %collective-permute-done.9 = bf16[256,1024]{1,0:T(8,128)(2,1)S(1)} collective-permute-done((bf16[256,1024]{1,0:T(8,128)(2,1)S(1)}, bf16[256,1024]{1,0:T(8,128)(2,1)S(1)}, u32[]{:S(2)}, u32[]{:S(2)}) %collective-permute-start.9) | collective-permute-done | bytes 524320 | tf_op jit(solution)/shard_map/ppermute | solution.py:44
  65.0 2.0 %collective-permute-start.10 = (bf16[256,1024]{1,0:T(8,128)(2,1)S(1)}, bf16[256,1024]{1,0:T(8,128)(2,1)S(1)}, u32[]{:S(2)}, u32[]{:S(2)}) collective-permute-start(bf16[256,1024]{1,0:T(8,128)(2,1)S(1)} %collective-permute-done.9), channel_id=1, source_target_pairs={{0,192},{1,49},{2,194},{3,51},{4,196},{5,53},{6,198},{7,55},{8,200... | collective-permute-start | bytes 1572872 | tf_op jit(solution)/shard_map/ppermute | solution.py:44
  67.0 0.8 collective-permute-start.5
  67.8 0.0 collective-permute-done.3.refs_1_
  67.8 0.6 collective-permute-start.4
  68.4 9.4 %collective-permute-done.7 = bf16[256,1024]{1,0:T(8,128)(2,1)S(1)} collective-permute-done((bf16[256,1024]{1,0:T(8,128)(2,1)S(1)}, bf16[256,1024]{1,0:T(8,128)(2,1)S(1)}, u32[]{:S(2)}, u32[]{:S(2)}) %collective-permute-start.7) | collective-permute-done | bytes 524320 | tf_op jit(solution)/shard_map/ppermute | solution.py:44
  77.8 2.4 %collective-permute-start.12 = (bf16[256,1024]{1,0:T(8,128)(2,1)S(1)}, bf16[256,1024]{1,0:T(8,128)(2,1)S(1)}, u32[]{:S(2)}, u32[]{:S(2)}) collective-permute-start(bf16[256,1024]{1,0:T(8,128)(2,1)S(1)} %collective-permute-done.9), channel_id=1, source_target_pairs={{0,1},{1,0},{2,3},{3,2},{4,5},{5,4},{6,7},{7,6},{8,9},{9,8},{10,11... | collective-permute-start | bytes 1572872 | tf_op jit(solution)/shard_map/ppermute | solution.py:48
  80.2 0.0 collective-permute-done.6.refs_0_
  80.2 0.0 collective-permute-start.8
  80.2 0.0 collective-permute-done.10
  80.2 0.5 collective-permute-start.11
  80.7 0.1 shard_map.49.near_ref
  80.8 0.9 collective-permute-done.12.refs_3_
  81.7 0.7 collective-permute-done.8.refs_1_
  82.5 0.7 collective-permute-done.11.refs_2_
  83.2 0.1 shard_map.50.panel_ref
  83.4 0.0 copy-start
  83.4 1.3 %copy-done = bf16[1024,1024]{1,0:T(8,128)(2,1)} copy-done((bf16[1024,1024]{1,0:T(8,128)(2,1)}, bf16[1024,1024]{1,0:T(8,128)(2,1)S(1)}, u32[]{:S(2)}) %copy-start) | copy-done | bytes 2097176
  84.7 0.0 copy-start.6
  84.7 0.3 collective-permute-done.5.refs_3_
  85.0 1.0 collective-permute-done.4.refs_2_
  85.9 0.1 shard_map.51
  86.0 0.0 copy-start.2
  86.0 1.0 copy-done.2
  87.0 0.0 all-to-all-done.1
  87.0 0.0 copy-start.1
  87.0 2.0 %collective-permute-start.13 = (bf16[1024,1024]{1,0:T(8,128)(2,1)S(1)}, bf16[1024,1024]{1,0:T(8,128)(2,1)S(1)}, u32[]{:S(2)}, u32[]{:S(2)}) collective-permute-start(bf16[1024,1024]{1,0:T(8,128)(2,1)S(1)} %bitcast.9), channel_id=1, source_target_pairs={{0,1},{1,0},{2,3},{3,2},{4,5},{5,4},{6,7},{7,6},{8,9},{9,8},{10,11... | collective-permute-start | bytes 6291464 | tf_op jit(solution)/shard_map/ppermute | solution.py:48
  89.0 0.0 copy-done.6
  89.0 0.0 copy-start.3
  89.0 1.2 %copy-done.3 = bf16[512,1024]{1,0:T(8,128)(2,1)S(1)} copy-done((bf16[512,1024]{1,0:T(8,128)(2,1)S(1)}, bf16[512,1024]{1,0:T(8,128)(2,1)}, u32[]{:S(2)}) %copy-start.3) | copy-done | bytes 1048600
  90.2 0.0 copy-start.4
  90.2 0.0 copy-start.5
  90.2 2.9 %shard_map.52.total_ref = f32[1024,1024]{1,0:T(8,128)S(1)} custom-call(s32[4]{0:T(128)S(1)} %copy-done.6, bf16[1024,1024]{1,0:T(8,128)(2,1)S(1)} %bitcast.10, bf16[512,1024]{1,0:T(8,128)(2,1)S(1)} %shard_map.49.near_ref, bf16[512,1024]{1,0:T(8,128)(2,1)S(1)} %copy-done.3), custom_call_target="tpu_custom_call" | custom-call | flops 2147483648 | bytes 8388608 | tf_op jit(solution)/shard_map/pallas_call | solution.py:195
  93.2 0.0 collective-permute-done.13.rows_ref
  93.2 0.0 copy-done.1
  93.2 0.0 copy-done.4
  93.2 0.0 copy-done.5
  93.2 5.1 %shard_map.53 = bf16[1024,2,512]{2,1,0:T(2,128)(2,1)} custom-call(s32[4]{0:T(128)S(1)} %copy-done.6, bf16[1024,1024]{1,0:T(8,128)(2,1)S(1)} %collective-permute-done.13.rows_ref, bf16[1024,1024]{1,0:T(8,128)(2,1)S(1)} %copy-done.1, f32[1024,1024]{1,0:T(8,128)S(1)} %shard_map.52.total_ref, f32[1,1024]{1,0:T(1,128)S(1)} %get-tuple-element.30.col_len_ref, ...), custom_call_target="tpu_custom_call" | custom-call | flops 2147483648 | bytes 8388608 | tf_op jit(solution)/shard_map/pallas_call | solution.py:241
  (1 shorter events, 0.0 us)
Async XLA Ops:
  22.7 64.3 %all-to-all-start.1 = ((bf16[8,128,1024]{2,0,1:T(8,128)(2,1)}), bf16[8,128,1024]{2,0,1:T(8,128)(2,1)S(1)}, u32[]{:S(2)}, u32[]{:S(2)}) async-start(bf16[8,128,1024]{2,0,1:T(8,128)(2,1)} %bitcast.12), calls=%async_computation.1 | async-start | bytes 4194304 | tf_op jit(solution)/shard_map/all_to_all | solution.py:263
  33.2 11.6 %collective-permute-start = (bf16[64,2176]{1,0:T(8,128)(2,1)S(1)}, bf16[64,2176]{1,0:T(8,128)(2,1)S(1)}, u32[]{:S(2)}, u32[]{:S(2)}) collective-permute-start(bf16[64,2176]{1,0:T(8,128)(2,1)S(1)} %shard_map.47.a_ref), channel_id=1, source_target_pairs={{0,16},{1,65},{2,18},{3,67},{4,20},{5,69},{6,22},{7,71},{8,24},{9,... | collective-permute-start | bytes 835592 | tf_op jit(solution)/shard_map/ppermute | solution.py:44
  34.0 17.6 %collective-permute-start.1 = (bf16[64,2176]{1,0:T(8,128)(2,1)S(1)}, bf16[64,2176]{1,0:T(8,128)(2,1)S(1)}, u32[]{:S(2)}, u32[]{:S(2)}) collective-permute-start(bf16[64,2176]{1,0:T(8,128)(2,1)S(1)} %shard_map.47.a_ref), channel_id=1, source_target_pairs={{0,32},{1,129},{2,34},{3,131},{4,36},{5,133},{6,38},{7,135},{8,40}... | collective-permute-start | bytes 835592 | tf_op jit(solution)/shard_map/ppermute | solution.py:44
  36.8 14.7 %collective-permute-start.2 = (bf16[64,2176]{1,0:T(8,128)(2,1)S(1)}, bf16[64,2176]{1,0:T(8,128)(2,1)S(1)}, u32[]{:S(2)}, u32[]{:S(2)}) collective-permute-start(bf16[64,2176]{1,0:T(8,128)(2,1)S(1)} %shard_map.47.a_ref), channel_id=1, source_target_pairs={{0,48},{1,193},{2,50},{3,195},{4,52},{5,197},{6,54},{7,199},{8,56}... | collective-permute-start | bytes 835592 | tf_op jit(solution)/shard_map/ppermute | solution.py:44
  51.6 13.4 %collective-permute-start.9 = (bf16[256,1024]{1,0:T(8,128)(2,1)S(1)}, bf16[256,1024]{1,0:T(8,128)(2,1)S(1)}, u32[]{:S(2)}, u32[]{:S(2)}) collective-permute-start(bf16[256,1024]{1,0:T(8,128)(2,1)S(1)} %get-tuple-element.21), channel_id=1, source_target_pairs={{0,192},{1,49},{2,194},{3,51},{4,196},{5,53},{6,198},{7,55},{8,200... | collective-permute-start | bytes 1572872 | tf_op jit(solution)/shard_map/ppermute | solution.py:44
  53.2 14.6 %collective-permute-start.3 = (bf16[272,1024]{1,0:T(8,128)(2,1)S(1)}, bf16[272,1024]{1,0:T(8,128)(2,1)S(1)}, u32[]{:S(2)}, u32[]{:S(2)}) collective-permute-start(bf16[272,1024]{1,0:T(8,128)(2,1)S(1)} %get-tuple-element.20.refs_0_), channel_id=1, source_target_pairs={{0,64},{1,17},{2,66},{3,19},{4,68},{5,21},{6,70},{7,23},{8,72},{9,... | collective-permute-start | bytes 1671176 | tf_op jit(solution)/shard_map/ppermute | solution.py:44
  53.4 24.4 %collective-permute-start.7 = (bf16[256,1024]{1,0:T(8,128)(2,1)S(1)}, bf16[256,1024]{1,0:T(8,128)(2,1)S(1)}, u32[]{:S(2)}, u32[]{:S(2)}) collective-permute-start(bf16[256,1024]{1,0:T(8,128)(2,1)S(1)} %get-tuple-element.21), channel_id=1, source_target_pairs={{0,64},{1,17},{2,66},{3,19},{4,68},{5,21},{6,70},{7,23},{8,72},{9,... | collective-permute-start | bytes 1572872 | tf_op jit(solution)/shard_map/ppermute | solution.py:44
  54.8 25.4 %collective-permute-start.6 = (bf16[256,1024]{1,0:T(8,128)(2,1)S(1)}, bf16[256,1024]{1,0:T(8,128)(2,1)S(1)}, u32[]{:S(2)}, u32[]{:S(2)}) collective-permute-start(bf16[256,1024]{1,0:T(8,128)(2,1)S(1)} %get-tuple-element.21), channel_id=1, source_target_pairs={{0,1},{1,0},{2,3},{3,2},{4,5},{5,4},{6,7},{7,6},{8,9},{9,8},{10,11... | collective-permute-start | bytes 1572872 | tf_op jit(solution)/shard_map/ppermute | solution.py:48
  65.0 15.2 %collective-permute-start.10 = (bf16[256,1024]{1,0:T(8,128)(2,1)S(1)}, bf16[256,1024]{1,0:T(8,128)(2,1)S(1)}, u32[]{:S(2)}, u32[]{:S(2)}) collective-permute-start(bf16[256,1024]{1,0:T(8,128)(2,1)S(1)} %collective-permute-done.9), channel_id=1, source_target_pairs={{0,192},{1,49},{2,194},{3,51},{4,196},{5,53},{6,198},{7,55},{8,200... | collective-permute-start | bytes 1572872 | tf_op jit(solution)/shard_map/ppermute | solution.py:44
  67.0 18.0 %collective-permute-start.5 = (bf16[272,1024]{1,0:T(8,128)(2,1)S(1)}, bf16[272,1024]{1,0:T(8,128)(2,1)S(1)}, u32[]{:S(2)}, u32[]{:S(2)}) collective-permute-start(bf16[272,1024]{1,0:T(8,128)(2,1)S(1)} %get-tuple-element.20.refs_0_), channel_id=1, source_target_pairs={{0,192},{1,49},{2,194},{3,51},{4,196},{5,53},{6,198},{7,55},{8,200... | collective-permute-start | bytes 1671176 | tf_op jit(solution)/shard_map/ppermute | solution.py:44
  67.8 18.1 %collective-permute-start.4 = (bf16[272,1024]{1,0:T(8,128)(2,1)S(1)}, bf16[272,1024]{1,0:T(8,128)(2,1)S(1)}, u32[]{:S(2)}, u32[]{:S(2)}) collective-permute-start(bf16[272,1024]{1,0:T(8,128)(2,1)S(1)} %collective-permute-done.3.refs_1_), channel_id=1, source_target_pairs={{0,64},{1,17},{2,66},{3,19},{4,68},{5,21},{6,70},{7,23},{8,72},{9,... | collective-permute-start | bytes 1671176 | tf_op jit(solution)/shard_map/ppermute | solution.py:44
  77.8 3.9 %collective-permute-start.12 = (bf16[256,1024]{1,0:T(8,128)(2,1)S(1)}, bf16[256,1024]{1,0:T(8,128)(2,1)S(1)}, u32[]{:S(2)}, u32[]{:S(2)}) collective-permute-start(bf16[256,1024]{1,0:T(8,128)(2,1)S(1)} %collective-permute-done.9), channel_id=1, source_target_pairs={{0,1},{1,0},{2,3},{3,2},{4,5},{5,4},{6,7},{7,6},{8,9},{9,8},{10,11... | collective-permute-start | bytes 1572872 | tf_op jit(solution)/shard_map/ppermute | solution.py:48
  80.2 2.3 %collective-permute-start.8 = (bf16[256,1024]{1,0:T(8,128)(2,1)S(1)}, bf16[256,1024]{1,0:T(8,128)(2,1)S(1)}, u32[]{:S(2)}, u32[]{:S(2)}) collective-permute-start(bf16[256,1024]{1,0:T(8,128)(2,1)S(1)} %collective-permute-done.7), channel_id=1, source_target_pairs={{0,1},{1,0},{2,3},{3,2},{4,5},{5,4},{6,7},{7,6},{8,9},{9,8},{10,11... | collective-permute-start | bytes 1572872 | tf_op jit(solution)/shard_map/ppermute | solution.py:48
  80.2 3.0 %collective-permute-start.11 = (bf16[256,1024]{1,0:T(8,128)(2,1)S(1)}, bf16[256,1024]{1,0:T(8,128)(2,1)S(1)}, u32[]{:S(2)}, u32[]{:S(2)}) collective-permute-start(bf16[256,1024]{1,0:T(8,128)(2,1)S(1)} %collective-permute-done.10), channel_id=1, source_target_pairs={{0,1},{1,0},{2,3},{3,2},{4,5},{5,4},{6,7},{7,6},{8,9},{9,8},{10,11... | collective-permute-start | bytes 1572872 | tf_op jit(solution)/shard_map/ppermute | solution.py:48
  83.4 1.3 %copy-start = (bf16[1024,1024]{1,0:T(8,128)(2,1)}, bf16[1024,1024]{1,0:T(8,128)(2,1)S(1)}, u32[]{:S(2)}) copy-start(bf16[1024,1024]{1,0:T(8,128)(2,1)S(1)} %shard_map.50.panel_ref) | copy-start | bytes 6291460
  84.7 4.3 %copy-start.6 = (s32[4]{0:T(128)S(1)}, s32[4]{0:T(128)}, u32[]{:S(2)}) copy-start(s32[4]{0:T(128)} %pad_add_fusion.place_ref.at_ref) | copy-start | bytes 52
  86.0 1.0 %copy-start.2 = (bf16[512,1024]{1,0:T(8,128)(2,1)}, bf16[512,1024]{1,0:T(8,128)(2,1)S(1)}, u32[]{:S(2)}) copy-start(bf16[512,1024]{1,0:T(8,128)(2,1)S(1)} %get-tuple-element.29.rest_ref) | copy-start | bytes 3145732
  87.0 6.2 %copy-start.1 = (bf16[1024,1024]{1,0:T(8,128)(2,1)S(1)}, bf16[1024,1024]{1,0:T(8,128)(2,1)}, u32[]{:S(2)}) copy-start(bf16[1024,1024]{1,0:T(8,128)(2,1)} %copy-done) | copy-start | bytes 6291460
  87.0 6.2 %collective-permute-start.13 = (bf16[1024,1024]{1,0:T(8,128)(2,1)S(1)}, bf16[1024,1024]{1,0:T(8,128)(2,1)S(1)}, u32[]{:S(2)}, u32[]{:S(2)}) collective-permute-start(bf16[1024,1024]{1,0:T(8,128)(2,1)S(1)} %bitcast.9), channel_id=1, source_target_pairs={{0,1},{1,0},{2,3},{3,2},{4,5},{5,4},{6,7},{7,6},{8,9},{9,8},{10,11... | collective-permute-start | bytes 6291464 | tf_op jit(solution)/shard_map/ppermute | solution.py:48
  89.0 1.2 %copy-start.3 = (bf16[512,1024]{1,0:T(8,128)(2,1)S(1)}, bf16[512,1024]{1,0:T(8,128)(2,1)}, u32[]{:S(2)}) copy-start(bf16[512,1024]{1,0:T(8,128)(2,1)} %copy-done.2) | copy-start | bytes 3145732
  90.2 3.0 %copy-start.4 = (s32[1024]{0:T(1024)S(1)}, s32[1024]{0:T(1024)}, u32[]{:S(2)}) copy-start(s32[1024]{0:T(1024)} %len_ref.1) | copy-start | bytes 12292
  90.2 3.0 %copy-start.5 = (s32[2,8,8]{2,1,0:T(8,128)S(1)}, s32[2,8,8]{2,1,0:T(8,128)}, u32[]{:S(2)}) copy-start(s32[2,8,8]{2,1,0:T(8,128)} %mask_ref.1) | copy-start | bytes 1540

commit v4 on v3

--- a/solution.py
+++ b/solution.py
@@ -151,8 +151,7 @@
 
 def pack_last_kernel(*refs):
     panels, (rest_ref, len_ref) = refs[:4], refs[4:]
-    for i in range(2):
-        rest_ref[i * GROUP : (i + 1) * GROUP] = panels[2 + i][:GROUP]
+    rest_ref[...] = panels[2][:GROUP]
     lens = sum(ref[GROUP:, :BLK].astype(jnp.float32) for ref in panels)
     lens = lens[:8] * 256 + lens[8:]
     len_ref[...] = jnp.concatenate([lens[j : j + 1] for j in range(8)], axis=1)
@@ -164,7 +163,7 @@
         in_specs=[VMEM] * 4,
         out_specs=[VMEM] * 2,
         out_shape=[
-            jax.ShapeDtypeStruct((2 * GROUP, WIDTH), jnp.bfloat16),
+            jax.ShapeDtypeStruct((GROUP, WIDTH), jnp.bfloat16),
             jax.ShapeDtypeStruct((1, WIDTH), jnp.float32),
         ],
         compiler_params=params(6),
@@ -188,7 +187,7 @@
 def first_kernel(at_ref, rows_ref, near_ref, rest_ref, out_ref):
     for i in range(PANEL // ROWS):
         columns = slice(i * ROWS, (i + 1) * ROWS)
-        out_ref[columns, :] = product(at_ref, rows_ref, (near_ref, rest_ref), at_ref[1] == 0, columns)
+        out_ref[columns, :] = product(at_ref, rows_ref, (near_ref.at[: 2 * GROUP], rest_ref, near_ref.at[2 * GROUP :]), at_ref[1] == 0, columns)
 
 
 def first_dot(place, local, near, rest):
@@ -269,9 +268,9 @@
     mine_far, other_far = shift(mine_up, 1, 1), shift(other_down, 1, -1)
     panels = [mine, mine_up, mine_far, mine_down]
     swapped = [swap(a) for a in (other, other_up, other_far, other_down)]
-    near = pack(*panels[:2])
+    near = pack(panels[0], panels[1], panels[3])
     other_panel = pack(*swapped)
-    panels[3], other_panel = lax.optimization_barrier((panels[3], other_panel))
+    panels[2], other_panel, near = lax.optimization_barrier((panels[2], other_panel, near))
     rest, col_len = pack_last(*panels)
     local, near, rest, other_panel, col_len = lax.optimization_barrier((local, near, rest, other_panel, col_len))
     remote = swap(local)

time: 98.9 us -> 98.6 us (level)
  waiting for transfers between devices: 36.7 us -> 33.8 us
  starting transfers between devices: 26.9 us -> 29.1 us
    ppermute x5, starting transfers between devices: 5.21 us -> 7.86 us  [swap(): return lax.ppermute(value, 'kmer', SWAP)]
    ppermute x5, waiting for transfers between devices: 2.45 us -> 0.27 us  [swap(): return lax.ppermute(value, 'kmer', SWAP)]
  transfers between devices with their start and end apart: 15 -> 15, of which waited for: 9 -> 7; matrix products, arithmetic and copies ran while one was open for 0% -> 0% of each run, Pallas kernels for 3% -> 3%
where the time goes in v4:
time: 98.6 us; the launch traced here: 98.2 us
  waiting for transfers between devices  33.8 us (34%)
  starting transfers between devices  29.1 us (30%)
  blocking collectives  19.9 us (20%)
  Pallas kernels  10.7 us (11%)
  local copies, waits for them, and re-layouts  3.89 us (4%)
    ppermute x9, waiting for transfers between devices, shift(): return lax.ppermute(value, ('seq', 'kmer'), pairs)  33.5 us
    all_to_all x1, blocking collectives, shards(): lax.all_to_all(piece, 'seq', 0, 0, axis_index_groups=LINES, tiled=True)  19.9 us
    ppermute x9, starting transfers between devices, shift(): return lax.ppermute(value, ('seq', 'kmer'), pairs)  10.8 us
    all_to_all x1, starting transfers between devices, shards(): lax.all_to_all(profiles, 'seq', split_axis=1, concat_axis=0, tiled=True)  10.5 us
    ppermute x5, starting transfers between devices, swap(): return lax.ppermute(value, 'kmer', SWAP)  7.86 us
    pallas_call x1, Pallas kernels, second_dot(): pl.pallas_call(second_kernel, in_specs=[SMEM] + [VMEM] * 6, out_specs=pl....  5.14 us
    unnamed x14, local copies, waits for them, and re-layouts  3.89 us
    pallas_call x1, Pallas kernels, first_dot(): pl.pallas_call(first_kernel, in_specs=[SMEM] + [VMEM] * 3, out_specs=VMEM...  2.96 us
  transfers between devices with their start and end apart: 15, of which 7 were waited for; matrix products, arithmetic and copies ran while one was open for 0% of the time, Pallas kernels for 3%

profile of v4, /device:TPU:1, one launch (start us, length us, event | category | flops | bytes accessed | tf_op | source)
XLA Modules:
  0.0 98.2 jit_solution(17794189025366510608)
XLA Ops:
  0.0 0.7 pad_add_fusion.place_ref.at_ref
  0.7 2.2 %shard_map.46 = bf16[8,8,2304]{2,1,0:T(8,128)(2,1)} custom-call(s32[2]{0:T(128)} %own_ref.1, s32[4]{0:T(128)} %pad_add_fusion.place_ref.at_ref, bf16[8,131072]{1,0:T(8,128)(2,1)} %d_ref.1, bf16[8,131072]{1,0:T(8,128)(2,1)} %d_ref.1, bf16[8,131072]{1,0:T(8,128)(2,1)} %d_ref.1, bf16[8,131072]{1,0:T(8,128)(2,1)} %d_ref.1, s32[1024]{0:T(1024)} %len_ref.1), custom_call_target="tpu_custom_call" | custom-call | tf_op jit(solution)/shard_map/pallas_call | solution.py:76
  2.8 19.9 %all_to_all.24.line_ref = bf16[8,8,2304]{2,1,0:T(8,128)(2,1)S(1)} all-to-all(bf16[8,8,2304]{2,1,0:T(8,128)(2,1)} %shard_map.46), channel_id=1, replica_groups={{0,2,4,6,8,10,12,14},{16,18,20,22,24,26,28,30},{32,34,36,38,40,42,44,46..., dimensions={0} | all-to-all | bytes 589824 | tf_op jit(solution)/shard_map/all_to_all | solution.py:260
  22.7 10.5 %all-to-all-start.1 = ((bf16[8,128,1024]{2,0,1:T(8,128)(2,1)}), bf16[8,128,1024]{2,0,1:T(8,128)(2,1)S(1)}, u32[]{:S(2)}, u32[]{:S(2)}) async-start(bf16[8,128,1024]{2,0,1:T(8,128)(2,1)} %bitcast.12), calls=%async_computation.1 | async-start | bytes 4194304 | tf_op jit(solution)/shard_map/all_to_all | solution.py:262
  33.2 0.8 collective-permute-start
  34.0 2.8 %collective-permute-start.1 = (bf16[64,2176]{1,0:T(8,128)(2,1)S(1)}, bf16[64,2176]{1,0:T(8,128)(2,1)S(1)}, u32[]{:S(2)}, u32[]{:S(2)}) collective-permute-start(bf16[64,2176]{1,0:T(8,128)(2,1)S(1)} %shard_map.47.a_ref), channel_id=1, source_target_pairs={{0,32},{1,129},{2,34},{3,131},{4,36},{5,133},{6,38},{7,135},{8,40}... | collective-permute-start | bytes 835592 | tf_op jit(solution)/shard_map/ppermute | solution.py:44
  36.8 1.0 collective-permute-start.2
  37.8 7.1 %collective-permute-done.b_ref = bf16[64,2176]{1,0:T(8,128)(2,1)S(1)} collective-permute-done((bf16[64,2176]{1,0:T(8,128)(2,1)S(1)}, bf16[64,2176]{1,0:T(8,128)(2,1)S(1)}, u32[]{:S(2)}, u32[]{:S(2)}) %collective-permute-start) | collective-permute-done | bytes 278560 | tf_op jit(solution)/shard_map/ppermute | solution.py:44
  44.8 6.7 %collective-permute-done.1.c_ref = bf16[64,2176]{1,0:T(8,128)(2,1)S(1)} collective-permute-done((bf16[64,2176]{1,0:T(8,128)(2,1)S(1)}, bf16[64,2176]{1,0:T(8,128)(2,1)S(1)}, u32[]{:S(2)}, u32[]{:S(2)}) %collective-permute-start.1) | collective-permute-done | bytes 278560 | tf_op jit(solution)/shard_map/ppermute | solution.py:44
  51.5 0.0 collective-permute-done.2.d_ref
  51.5 0.1 shard_map.48
  51.6 1.6 %collective-permute-start.8 = (bf16[256,1024]{1,0:T(8,128)(2,1)S(1)}, bf16[256,1024]{1,0:T(8,128)(2,1)S(1)}, u32[]{:S(2)}, u32[]{:S(2)}) collective-permute-start(bf16[256,1024]{1,0:T(8,128)(2,1)S(1)} %get-tuple-element.22), channel_id=1, source_target_pairs={{0,192},{1,49},{2,194},{3,51},{4,196},{5,53},{6,198},{7,55},{8,200... | collective-permute-start | bytes 1572872 | tf_op jit(solution)/shard_map/ppermute | solution.py:44
  53.2 0.2 collective-permute-start.3
  53.4 2.4 %collective-permute-start.12 = (bf16[272,1024]{1,0:T(8,128)(2,1)S(1)}, bf16[272,1024]{1,0:T(8,128)(2,1)S(1)}, u32[]{:S(2)}, u32[]{:S(2)}) collective-permute-start(bf16[272,1024]{1,0:T(8,128)(2,1)S(1)} %get-tuple-element.21.refs_0_), channel_id=1, source_target_pairs={{0,192},{1,49},{2,194},{3,51},{4,196},{5,53},{6,198},{7,55},{8,200... | collective-permute-start | bytes 1671176 | tf_op jit(solution)/shard_map/ppermute | solution.py:44
  55.9 0.0 collective-permute-start.6
  55.9 9.1 %collective-permute-done.8 = bf16[256,1024]{1,0:T(8,128)(2,1)S(1)} collective-permute-done((bf16[256,1024]{1,0:T(8,128)(2,1)S(1)}, bf16[256,1024]{1,0:T(8,128)(2,1)S(1)}, u32[]{:S(2)}, u32[]{:S(2)}) %collective-permute-start.8) | collective-permute-done | bytes 524320 | tf_op jit(solution)/shard_map/ppermute | solution.py:44
  65.0 2.0 %collective-permute-start.9 = (bf16[256,1024]{1,0:T(8,128)(2,1)S(1)}, bf16[256,1024]{1,0:T(8,128)(2,1)S(1)}, u32[]{:S(2)}, u32[]{:S(2)}) collective-permute-start(bf16[256,1024]{1,0:T(8,128)(2,1)S(1)} %collective-permute-done.8), channel_id=1, source_target_pairs={{0,192},{1,49},{2,194},{3,51},{4,196},{5,53},{6,198},{7,55},{8,200... | collective-permute-start | bytes 1572872 | tf_op jit(solution)/shard_map/ppermute | solution.py:44
  67.0 0.4 collective-permute-done.3.refs_1_
  67.3 0.0 collective-permute-start.4
  67.3 3.2 %collective-permute-start.5 = (bf16[256,1024]{1,0:T(8,128)(2,1)S(1)}, bf16[256,1024]{1,0:T(8,128)(2,1)S(1)}, u32[]{:S(2)}, u32[]{:S(2)}) collective-permute-start(bf16[256,1024]{1,0:T(8,128)(2,1)S(1)} %get-tuple-element.22), channel_id=1, source_target_pairs={{0,1},{1,0},{2,3},{3,2},{4,5},{5,4},{6,7},{7,6},{8,9},{9,8},{10,11... | collective-permute-start | bytes 1572872 | tf_op jit(solution)/shard_map/ppermute | solution.py:48
  70.5 7.3 %collective-permute-done.6 = bf16[256,1024]{1,0:T(8,128)(2,1)S(1)} collective-permute-done((bf16[256,1024]{1,0:T(8,128)(2,1)S(1)}, bf16[256,1024]{1,0:T(8,128)(2,1)S(1)}, u32[]{:S(2)}, u32[]{:S(2)}) %collective-permute-start.6) | collective-permute-done | bytes 524320 | tf_op jit(solution)/shard_map/ppermute | solution.py:44
  77.8 2.4 %collective-permute-start.11 = (bf16[256,1024]{1,0:T(8,128)(2,1)S(1)}, bf16[256,1024]{1,0:T(8,128)(2,1)S(1)}, u32[]{:S(2)}, u32[]{:S(2)}) collective-permute-start(bf16[256,1024]{1,0:T(8,128)(2,1)S(1)} %collective-permute-done.8), channel_id=1, source_target_pairs={{0,1},{1,0},{2,3},{3,2},{4,5},{5,4},{6,7},{7,6},{8,9},{9,8},{10,11... | collective-permute-start | bytes 1572872 | tf_op jit(solution)/shard_map/ppermute | solution.py:48
  80.2 0.0 collective-permute-done.12.refs_2_.refs_3_
  80.2 0.0 collective-permute-start.7
  80.2 3.0 %collective-permute-done.9 = bf16[256,1024]{1,0:T(8,128)(2,1)S(1)} collective-permute-done((bf16[256,1024]{1,0:T(8,128)(2,1)S(1)}, bf16[256,1024]{1,0:T(8,128)(2,1)S(1)}, u32[]{:S(2)}, u32[]{:S(2)}) %collective-permute-start.9) | collective-permute-done | bytes 524320 | tf_op jit(solution)/shard_map/ppermute | solution.py:44
  83.2 0.7 collective-permute-start.10
  83.9 0.1 shard_map.50.near_ref
  84.0 0.0 copy-start.2
  84.0 1.1 %copy-done.2 = bf16[768,1024]{1,0:T(8,128)(2,1)} copy-done((bf16[768,1024]{1,0:T(8,128)(2,1)}, bf16[768,1024]{1,0:T(8,128)(2,1)S(1)}, u32[]{:S(2)}) %copy-start.2) | copy-done | bytes 1572888
  85.1 0.0 collective-permute-done.5.refs_0_
  85.1 0.0 collective-permute-done.11.refs_3_
  85.1 0.0 collective-permute-done.7.refs_1_
  85.2 0.3 collective-permute-done.10.refs_2_
  85.4 0.1 shard_map.49.panel_ref
  85.6 0.0 copy-start
  85.6 1.3 %copy-done = bf16[1024,1024]{1,0:T(8,128)(2,1)} copy-done((bf16[1024,1024]{1,0:T(8,128)(2,1)}, bf16[1024,1024]{1,0:T(8,128)(2,1)S(1)}, u32[]{:S(2)}) %copy-start) | copy-done | bytes 2097176
  86.9 0.0 copy-start.6
  86.9 0.0 collective-permute-done.4.refs_2_
  86.9 0.0 all-to-all-done.1
  86.9 0.0 copy-start.1
  87.0 1.6 %collective-permute-start.13 = (bf16[1024,1024]{1,0:T(8,128)(2,1)S(1)}, bf16[1024,1024]{1,0:T(8,128)(2,1)S(1)}, u32[]{:S(2)}, u32[]{:S(2)}) collective-permute-start(bf16[1024,1024]{1,0:T(8,128)(2,1)S(1)} %bitcast.9), channel_id=1, source_target_pairs={{0,1},{1,0},{2,3},{3,2},{4,5},{5,4},{6,7},{7,6},{8,9},{9,8},{10,11... | collective-permute-start | bytes 6291464 | tf_op jit(solution)/shard_map/ppermute | solution.py:48
  88.5 0.0 copy-done.6
  88.5 0.0 copy-start.3
  88.5 1.4 %copy-done.3 = bf16[768,1024]{1,0:T(8,128)(2,1)S(1)} copy-done((bf16[768,1024]{1,0:T(8,128)(2,1)S(1)}, bf16[768,1024]{1,0:T(8,128)(2,1)}, u32[]{:S(2)}) %copy-start.3) | copy-done | bytes 1572888
  89.9 0.0 copy-start.4
  89.9 0.0 copy-start.5
  89.9 3.0 %shard_map.52.total_ref = f32[1024,1024]{1,0:T(8,128)S(1)} custom-call(s32[4]{0:T(128)S(1)} %copy-done.6, bf16[1024,1024]{1,0:T(8,128)(2,1)S(1)} %bitcast.10, bf16[768,1024]{1,0:T(8,128)(2,1)S(1)} %copy-done.3, bf16[256,1024]{1,0:T(8,128)(2,1)S(1)} %get-tuple-element.31.rest_ref), custom_call_target="tpu_custom_call" | custom-call | flops 2147483648 | bytes 8388608 | tf_op jit(solution)/shard_map/pallas_call | solution.py:194
  92.9 0.0 collective-permute-done.13.rows_ref
  92.9 0.0 copy-done.1
  92.9 0.0 copy-done.4
  92.9 0.0 copy-done.5
  92.9 5.1 %shard_map.53 = bf16[1024,2,512]{2,1,0:T(2,128)(2,1)} custom-call(s32[4]{0:T(128)S(1)} %copy-done.6, bf16[1024,1024]{1,0:T(8,128)(2,1)S(1)} %collective-permute-done.13.rows_ref, bf16[1024,1024]{1,0:T(8,128)(2,1)S(1)} %copy-done.1, f32[1024,1024]{1,0:T(8,128)S(1)} %shard_map.52.total_ref, f32[1,1024]{1,0:T(1,128)S(1)} %get-tuple-element.32.col_len_ref, ...), custom_call_target="tpu_custom_call" | custom-call | flops 2147483648 | bytes 8388608 | tf_op jit(solution)/shard_map/pallas_call | solution.py:240
  (2 shorter events, 0.1 us)
Async XLA Ops:
  22.7 64.3 %all-to-all-start.1 = ((bf16[8,128,1024]{2,0,1:T(8,128)(2,1)}), bf16[8,128,1024]{2,0,1:T(8,128)(2,1)S(1)}, u32[]{:S(2)}, u32[]{:S(2)}) async-start(bf16[8,128,1024]{2,0,1:T(8,128)(2,1)} %bitcast.12), calls=%async_computation.1 | async-start | bytes 4194304 | tf_op jit(solution)/shard_map/all_to_all | solution.py:262
  33.2 11.6 %collective-permute-start = (bf16[64,2176]{1,0:T(8,128)(2,1)S(1)}, bf16[64,2176]{1,0:T(8,128)(2,1)S(1)}, u32[]{:S(2)}, u32[]{:S(2)}) collective-permute-start(bf16[64,2176]{1,0:T(8,128)(2,1)S(1)} %shard_map.47.a_ref), channel_id=1, source_target_pairs={{0,16},{1,65},{2,18},{3,67},{4,20},{5,69},{6,22},{7,71},{8,24},{9,... | collective-permute-start | bytes 835592 | tf_op jit(solution)/shard_map/ppermute | solution.py:44
  34.0 17.6 %collective-permute-start.1 = (bf16[64,2176]{1,0:T(8,128)(2,1)S(1)}, bf16[64,2176]{1,0:T(8,128)(2,1)S(1)}, u32[]{:S(2)}, u32[]{:S(2)}) collective-permute-start(bf16[64,2176]{1,0:T(8,128)(2,1)S(1)} %shard_map.47.a_ref), channel_id=1, source_target_pairs={{0,32},{1,129},{2,34},{3,131},{4,36},{5,133},{6,38},{7,135},{8,40}... | collective-permute-start | bytes 835592 | tf_op jit(solution)/shard_map/ppermute | solution.py:44
  36.8 14.7 %collective-permute-start.2 = (bf16[64,2176]{1,0:T(8,128)(2,1)S(1)}, bf16[64,2176]{1,0:T(8,128)(2,1)S(1)}, u32[]{:S(2)}, u32[]{:S(2)}) collective-permute-start(bf16[64,2176]{1,0:T(8,128)(2,1)S(1)} %shard_map.47.a_ref), channel_id=1, source_target_pairs={{0,48},{1,193},{2,50},{3,195},{4,52},{5,197},{6,54},{7,199},{8,56}... | collective-permute-start | bytes 835592 | tf_op jit(solution)/shard_map/ppermute | solution.py:44
  51.6 13.4 %collective-permute-start.8 = (bf16[256,1024]{1,0:T(8,128)(2,1)S(1)}, bf16[256,1024]{1,0:T(8,128)(2,1)S(1)}, u32[]{:S(2)}, u32[]{:S(2)}) collective-permute-start(bf16[256,1024]{1,0:T(8,128)(2,1)S(1)} %get-tuple-element.22), channel_id=1, source_target_pairs={{0,192},{1,49},{2,194},{3,51},{4,196},{5,53},{6,198},{7,55},{8,200... | collective-permute-start | bytes 1572872 | tf_op jit(solution)/shard_map/ppermute | solution.py:44
  53.2 14.1 %collective-permute-start.3 = (bf16[272,1024]{1,0:T(8,128)(2,1)S(1)}, bf16[272,1024]{1,0:T(8,128)(2,1)S(1)}, u32[]{:S(2)}, u32[]{:S(2)}) collective-permute-start(bf16[272,1024]{1,0:T(8,128)(2,1)S(1)} %get-tuple-element.21.refs_0_), channel_id=1, source_target_pairs={{0,64},{1,17},{2,66},{3,19},{4,68},{5,21},{6,70},{7,23},{8,72},{9,... | collective-permute-start | bytes 1671176 | tf_op jit(solution)/shard_map/ppermute | solution.py:44
  53.4 26.8 %collective-permute-start.12 = (bf16[272,1024]{1,0:T(8,128)(2,1)S(1)}, bf16[272,1024]{1,0:T(8,128)(2,1)S(1)}, u32[]{:S(2)}, u32[]{:S(2)}) collective-permute-start(bf16[272,1024]{1,0:T(8,128)(2,1)S(1)} %get-tuple-element.21.refs_0_), channel_id=1, source_target_pairs={{0,192},{1,49},{2,194},{3,51},{4,196},{5,53},{6,198},{7,55},{8,200... | collective-permute-start | bytes 1671176 | tf_op jit(solution)/shard_map/ppermute | solution.py:44
  55.9 21.9 %collective-permute-start.6 = (bf16[256,1024]{1,0:T(8,128)(2,1)S(1)}, bf16[256,1024]{1,0:T(8,128)(2,1)S(1)}, u32[]{:S(2)}, u32[]{:S(2)}) collective-permute-start(bf16[256,1024]{1,0:T(8,128)(2,1)S(1)} %get-tuple-element.22), channel_id=1, source_target_pairs={{0,64},{1,17},{2,66},{3,19},{4,68},{5,21},{6,70},{7,23},{8,72},{9,... | collective-permute-start | bytes 1572872 | tf_op jit(solution)/shard_map/ppermute | solution.py:44
  65.0 18.2 %collective-permute-start.9 = (bf16[256,1024]{1,0:T(8,128)(2,1)S(1)}, bf16[256,1024]{1,0:T(8,128)(2,1)S(1)}, u32[]{:S(2)}, u32[]{:S(2)}) collective-permute-start(bf16[256,1024]{1,0:T(8,128)(2,1)S(1)} %collective-permute-done.8), channel_id=1, source_target_pairs={{0,192},{1,49},{2,194},{3,51},{4,196},{5,53},{6,198},{7,55},{8,200... | collective-permute-start | bytes 1572872 | tf_op jit(solution)/shard_map/ppermute | solution.py:44
  67.3 19.6 %collective-permute-start.4 = (bf16[272,1024]{1,0:T(8,128)(2,1)S(1)}, bf16[272,1024]{1,0:T(8,128)(2,1)S(1)}, u32[]{:S(2)}, u32[]{:S(2)}) collective-permute-start(bf16[272,1024]{1,0:T(8,128)(2,1)S(1)} %collective-permute-done.3.refs_1_), channel_id=1, source_target_pairs={{0,64},{1,17},{2,66},{3,19},{4,68},{5,21},{6,70},{7,23},{8,72},{9,... | collective-permute-start | bytes 1671176 | tf_op jit(solution)/shard_map/ppermute | solution.py:44
  67.3 17.8 %collective-permute-start.5 = (bf16[256,1024]{1,0:T(8,128)(2,1)S(1)}, bf16[256,1024]{1,0:T(8,128)(2,1)S(1)}, u32[]{:S(2)}, u32[]{:S(2)}) collective-permute-start(bf16[256,1024]{1,0:T(8,128)(2,1)S(1)} %get-tuple-element.22), channel_id=1, source_target_pairs={{0,1},{1,0},{2,3},{3,2},{4,5},{5,4},{6,7},{7,6},{8,9},{9,8},{10,11... | collective-permute-start | bytes 1572872 | tf_op jit(solution)/shard_map/ppermute | solution.py:48
  77.8 7.3 %collective-permute-start.11 = (bf16[256,1024]{1,0:T(8,128)(2,1)S(1)}, bf16[256,1024]{1,0:T(8,128)(2,1)S(1)}, u32[]{:S(2)}, u32[]{:S(2)}) collective-permute-start(bf16[256,1024]{1,0:T(8,128)(2,1)S(1)} %collective-permute-done.8), channel_id=1, source_target_pairs={{0,1},{1,0},{2,3},{3,2},{4,5},{5,4},{6,7},{7,6},{8,9},{9,8},{10,11... | collective-permute-start | bytes 1572872 | tf_op jit(solution)/shard_map/ppermute | solution.py:48
  80.2 5.0 %collective-permute-start.7 = (bf16[256,1024]{1,0:T(8,128)(2,1)S(1)}, bf16[256,1024]{1,0:T(8,128)(2,1)S(1)}, u32[]{:S(2)}, u32[]{:S(2)}) collective-permute-start(bf16[256,1024]{1,0:T(8,128)(2,1)S(1)} %collective-permute-done.6), channel_id=1, source_target_pairs={{0,1},{1,0},{2,3},{3,2},{4,5},{5,4},{6,7},{7,6},{8,9},{9,8},{10,11... | collective-permute-start | bytes 1572872 | tf_op jit(solution)/shard_map/ppermute | solution.py:48
  83.2 2.2 %collective-permute-start.10 = (bf16[256,1024]{1,0:T(8,128)(2,1)S(1)}, bf16[256,1024]{1,0:T(8,128)(2,1)S(1)}, u32[]{:S(2)}, u32[]{:S(2)}) collective-permute-start(bf16[256,1024]{1,0:T(8,128)(2,1)S(1)} %collective-permute-done.9), channel_id=1, source_target_pairs={{0,1},{1,0},{2,3},{3,2},{4,5},{5,4},{6,7},{7,6},{8,9},{9,8},{10,11... | collective-permute-start | bytes 1572872 | tf_op jit(solution)/shard_map/ppermute | solution.py:48
  84.0 1.2 %copy-start.2 = (bf16[768,1024]{1,0:T(8,128)(2,1)}, bf16[768,1024]{1,0:T(8,128)(2,1)S(1)}, u32[]{:S(2)}) copy-start(bf16[768,1024]{1,0:T(8,128)(2,1)S(1)} %shard_map.50.near_ref) | copy-start | bytes 4718596
  85.6 1.3 %copy-start = (bf16[1024,1024]{1,0:T(8,128)(2,1)}, bf16[1024,1024]{1,0:T(8,128)(2,1)S(1)}, u32[]{:S(2)}) copy-start(bf16[1024,1024]{1,0:T(8,128)(2,1)S(1)} %shard_map.49.panel_ref) | copy-start | bytes 6291460
  86.9 1.6 %copy-start.6 = (s32[4]{0:T(128)S(1)}, s32[4]{0:T(128)}, u32[]{:S(2)}) copy-start(s32[4]{0:T(128)} %pad_add_fusion.place_ref.at_ref) | copy-start | bytes 52
  86.9 6.0 %copy-start.1 = (bf16[1024,1024]{1,0:T(8,128)(2,1)S(1)}, bf16[1024,1024]{1,0:T(8,128)(2,1)}, u32[]{:S(2)}) copy-start(bf16[1024,1024]{1,0:T(8,128)(2,1)} %copy-done) | copy-start | bytes 6291460
  87.0 6.0 %collective-permute-start.13 = (bf16[1024,1024]{1,0:T(8,128)(2,1)S(1)}, bf16[1024,1024]{1,0:T(8,128)(2,1)S(1)}, u32[]{:S(2)}, u32[]{:S(2)}) collective-permute-start(bf16[1024,1024]{1,0:T(8,128)(2,1)S(1)} %bitcast.9), channel_id=1, source_target_pairs={{0,1},{1,0},{2,3},{3,2},{4,5},{5,4},{6,7},{7,6},{8,9},{9,8},{10,11... | collective-permute-start | bytes 6291464 | tf_op jit(solution)/shard_map/ppermute | solution.py:48
  88.5 1.4 %copy-start.3 = (bf16[768,1024]{1,0:T(8,128)(2,1)S(1)}, bf16[768,1024]{1,0:T(8,128)(2,1)}, u32[]{:S(2)}) copy-start(bf16[768,1024]{1,0:T(8,128)(2,1)} %copy-done.2) | copy-start | bytes 4718596
  89.9 3.0 %copy-start.4 = (s32[1024]{0:T(1024)S(1)}, s32[1024]{0:T(1024)}, u32[]{:S(2)}) copy-start(s32[1024]{0:T(1024)} %len_ref.1) | copy-start | bytes 12292
  89.9 3.0 %copy-start.5 = (s32[2,8,8]{2,1,0:T(8,128)S(1)}, s32[2,8,8]{2,1,0:T(8,128)}, u32[]{:S(2)}) copy-start(s32[2,8,8]{2,1,0:T(8,128)} %mask_ref.1) | copy-start | bytes 1540
